TPU v7x, 32 devices: a whole 2x2x4 slice. The times are simulated.
32 devices in a mesh: row: 4 (over x, core), col: 4 (over z), layer: 2 (over y).
Axes of the slice: x: 2, y: 2, z: 4, core: 2. Of those that a mesh axis runs over, the one named last changes fastest.
Arguments:
- values: bfloat16 [2048, 2048], P('row', 'col'), may hold values from 0.0099487305 to 1
- tile_mask: int32 [16, 16], P('row', 'col'), may hold values from 0 to 1, as said below
Outputs:
- clustered: float32 [2048, 2048], P('row', ('col', 'layer'))
Inputs may be any that keep to these rules, and one draw needn't show every extreme that they name: `tile_mask`: every diagonal tile is nonzero. The blocks of (16 / 4) x 4 tiles that one device holds each have at most 8 nonzero tiles and at least 4; the block in the first grid row and first grid column has exactly 8.
All inputs are finite; a program needn't handle non-finite values.
Results may differ from a plain program's by a relative error of at most 0.0065.
Values may be sent and summed in bfloat16 or wider, within the bound.
A program may use at most 128 MiB of HBM per device.

v0:
```python
import jax
import jax.numpy as jnp
from jax import lax
from jax.sharding import PartitionSpec as P


def broadcast(block, axis, source):
    block = jnp.where(lax.axis_index(axis) == source, block, jnp.zeros_like(block))
    return lax.psum(block, axis)


def shards(values, tile_mask):
    height, width = values.shape
    tiles_r, tiles_c = tile_mask.shape
    edge = height // tiles_r
    grid = (
        values.reshape(tiles_r, edge, tiles_c, edge)
        * tile_mask.astype(jnp.bfloat16)[:, None, :, None]
    )
    masked = grid.reshape(height, width)
    mass = lax.psum(jnp.sum(masked, axis=0, dtype=jnp.float32), "row")
    stochastic = (masked.astype(jnp.float32) / mass[None, :]).astype(jnp.bfloat16)
    n_row = lax.axis_size("row")
    n_col = lax.axis_size("col")
    n_layer = lax.axis_size("layer")
    per_layer = n_col // n_layer
    group = n_col // n_row
    layer_idx = lax.axis_index("layer")
    total = jnp.zeros((height, width), jnp.float32)
    for section in range(per_layer):
        source = layer_idx * per_layer + section
        offset = source % group * width
        portion = lax.dynamic_slice_in_dim(stochastic, offset, width, 0)
        right = broadcast(portion, "row", source // group)
        left = broadcast(stochastic, "col", source)
        total = total + jnp.dot(left, right, preferred_element_type=jnp.float32)
    expanded = lax.psum_scatter(total, "layer", scatter_dimension=1, tiled=True)
    inflated = expanded * expanded
    weight = lax.psum(jnp.sum(inflated, axis=0), "row")
    order = height * n_row
    return order * 1.0 * inflated / weight[None, :]


def solution(mesh):
    return jax.shard_map(
        shards,
        mesh=mesh,
        in_specs=(P("row", "col"), P("row", "col")),
        out_specs=P("row", ("col", "layer")),
        check_vma=False,
    )
```

profile of v0, /device:TPU:0, one launch (start us, length us, event | category | flops | bytes accessed | tf_op | source)
XLA Modules:
  0.0 148.7 jit_solution(3805011888927063571)
XLA Ops:
  6.5 0.0 copy-start.1
  6.5 0.0 all-reduce.7.cloned.1.call-start
  6.5 0.7 convert_element_type.10
  7.3 0.2 mul.27
  7.5 0.1 copy-done.1
  7.6 0.2 convert_reduce_fusion
  7.8 8.3 %psum.42 = f32[512]{0:T(512)S(1)} all-reduce(f32[512]{0:T(512)S(1)} %convert_reduce_fusion), channel_id=1, replica_groups=mesh['row'=4,'col'=4,'layer'=2] {'row'}, use_global_device_ids=true, to_apply=%region_1.0 | all-reduce | flops 512 | bytes 4096 | tf_op jit(solution)/shard_map/psum | solution.py:21
  16.1 1.0 broadcast_select_fusion
  17.1 1.2 broadcast_select_fusion.2
  18.4 0.0 all-reduce.7.cloned.1.call-update
  18.4 0.0 all-reduce.5.cloned.1.call-start
  18.4 0.7 all-reduce.5.cloned.1.call-update
  19.1 0.0 reduce-scatter.2.cloned.1.call-start
  19.2 35.8 %all-reduce.7.cloned.1.call-done = (bf16[512,512]{1,0:T(8,128)(2,1)}, bf16[512,512]{1,0:T(8,128)(2,1)}) async-done(((bf16[512,512]{1,0:T(8,128)(2,1)}, bf16[512,512]{1,0:T(8,128)(2,1)}), (bf16[512,512]{1,0:T(8,128)(2,1)}, bf16[512,512]{1,0:T(8,128)(2,1)})) %all-reduce.7.cloned.1.call-update) | async-done | bytes 1048592 | tf_op jit(solution)/shard_map/psum | solution.py:9
  55.0 55.2 %all-reduce.5.cloned.1.call-done = (bf16[512,512]{1,0:T(8,128)(2,1)}, bf16[512,512]{1,0:T(8,128)(2,1)}) async-done(((bf16[512,512]{1,0:T(8,128)(2,1)}, bf16[512,512]{1,0:T(8,128)(2,1)}), (bf16[512,512]{1,0:T(8,128)(2,1)}, bf16[512,512]{1,0:T(8,128)(2,1)})) %all-reduce.5.cloned.1.call-update) | async-done | bytes 1048592 | tf_op jit(solution)/shard_map/psum | solution.py:9
  110.2 0.0 copy-start.2
  110.2 0.0 copy-start.3
  110.2 1.7 %fusion.2 = f32[512,512]{1,0:T(8,128)S(1)} fusion(bf16[512,512]{1,0:T(8,128)(2,1)} %get-tuple-element.5, bf16[512,512]{1,0:T(8,128)(2,1)} %get-tuple-element.7), kind=kOutput, calls=%fused_computation.11 | convolution fusion | flops 268435456 | bytes 2097152 | tf_op jit(solution)/shard_map/dot_general | solution.py:36
  111.9 0.0 copy-done.2
  111.9 0.0 copy-done.3
  111.9 1.4 convolution_add_fusion
  113.4 0.0 reduce-scatter.2.cloned.1.call-update
  113.4 19.9 %reduce-scatter.2.cloned.1.call-done = f32[512,256]{1,0:T(8,128)} async-done(((f32[512,512]{1,0:T(8,128)}), f32[512,256]{1,0:T(8,128)}) %reduce-scatter.2.cloned.1.call-update) | async-done | bytes 524304 | tf_op jit(solution)/shard_map/reduce_scatter | solution.py:37
  133.2 0.0 copy-start
  133.2 1.2 multiply_reduce_fusion
  134.4 6.9 %psum.47 = f32[256]{0:T(256)S(1)} all-reduce(f32[256]{0:T(256)S(1)} %multiply_reduce_fusion), channel_id=1, replica_groups=mesh['row'=4,'col'=4,'layer'=2] {'row'}, use_global_device_ids=true, to_apply=%region_8.9 | all-reduce | flops 256 | bytes 2048 | tf_op jit(solution)/shard_map/psum | solution.py:39
  141.3 0.0 copy-done
  141.3 0.8 multiply_divide_fusion
Async XLA Ops:
  6.5 1.1 copy-start.1
  6.5 48.5 %all-reduce.7.cloned.1.call-start = ((), (), s32[]{:S(2)}) async-start(), calls=%async_computation.3 | async-start | bytes 2097152 | tf_op jit(solution)/shard_map/psum | solution.py:9
  18.4 91.8 %all-reduce.5.cloned.1.call-start = ((), (), s32[]{:S(2)}) async-start(), calls=%async_computation.2 | async-start | bytes 2097152 | tf_op jit(solution)/shard_map/psum | solution.py:9
  19.1 114.1 %reduce-scatter.2.cloned.1.call-start = ((), (), s32[]{:S(2)}) async-start(), calls=%async_computation.1 | async-start | bytes 1572864 | tf_op jit(solution)/shard_map/reduce_scatter | solution.py:37
  110.2 1.7 %copy-start.2 = (bf16[512,512]{1,0:T(8,128)(2,1)S(1)}, bf16[512,512]{1,0:T(8,128)(2,1)}, u32[]{:S(2)}) copy-start(bf16[512,512]{1,0:T(8,128)(2,1)} %get-tuple-element.8) | copy-start | bytes 1572868
  110.2 1.7 %copy-start.3 = (bf16[512,512]{1,0:T(8,128)(2,1)S(1)}, bf16[512,512]{1,0:T(8,128)(2,1)}, u32[]{:S(2)}) copy-start(bf16[512,512]{1,0:T(8,128)(2,1)} %get-tuple-element.6) | copy-start | bytes 1572868
  133.2 8.1 %copy-start = (f32[512,256]{1,0:T(8,128)S(1)}, f32[512,256]{1,0:T(8,128)}, u32[]{:S(2)}) copy-start(f32[512,256]{1,0:T(8,128)} %reduce-scatter.2.cloned.1.call-done) | copy-start | bytes 1572868
Sparse Core Ops, SparseCore 0:
  18.5 36.4 all-reduce.6
  57.5 52.5 all-reduce.4
  113.5 19.6 reduce-scatter.1
where the time goes:
time: 149 us
  waiting for transfers between devices  112 us (75%)
  blocking collectives  15.2 us (10%)
  between operations  13.1 us (9%)
  other arithmetic  5.22 us (4%)
  matrix products  3.15 us (2%)
    psum x2, waiting for transfers between devices, broadcast(): return lax.psum(block, axis)  91 us
    reduce_scatter x1, waiting for transfers between devices, shards(): expanded = lax.psum_scatter(total, 'layer', scatter_dimension=1, tiled=True)  19.9 us
    psum x1, blocking collectives, shards(): mass = lax.psum(jnp.sum(masked, axis=0, dtype=jnp.float32), 'row')  8.33 us
    psum x1, blocking collectives, shards(): weight = lax.psum(jnp.sum(inflated, axis=0), 'row')  6.86 us
    dot_general x2, matrix products, shards(): total = total + jnp.dot(left, right, preferred_element_type=jnp.float32)  3.15 us
  transfers between devices with their start and end apart: 3, of which 3 were waited for; matrix products, arithmetic and copies ran while one was open for 0% of the time, Pallas kernels for 0%

commit v1 on v0

v1 whole, which is shorter than its diff:
```python
import functools

import jax
import jax.numpy as jnp
from jax import lax
from jax.experimental import pallas as pl
from jax.experimental.pallas import tpu as pltpu
from jax.sharding import PartitionSpec as P

MESH = pl.DeviceIdType.MESH
EDGE = 128
CHUNKS = 2


def kernel(
    dims, v_ref, m_ref, infl_ref, scale_ref,
    by_tile, pack, rbuf, acc, mask_all, ranks, mpart, mass, wpart, *rest,
):
    n_row, n_col, n_layer, tiles_r, tiles_c, live = dims
    steps = n_col - 1
    from_left = rest[:steps]
    from_right = rest[steps : 2 * steps]
    (z_send, z_recv, y_send, y_recv, x_send, x_recv, mask_send, mask_recv,
     mp_send, mp_recv, ms_send, ms_recv, w_send, w_recv) = rest[2 * steps :]
    height, width = tiles_r * EDGE, tiles_c * EDGE
    half = width // n_layer
    half_tiles = tiles_c // n_layer
    tiles = tiles_r * tiles_c
    part = live // n_layer
    chunk = part // CHUNKS
    per = height // width
    r = lax.axis_index("row")
    c = lax.axis_index("col")
    l = lax.axis_index("layer")

    barrier = pltpu.get_barrier_semaphore()
    for axis, me, size in (("col", c, n_col), ("row", r, n_row), ("layer", l, n_layer)):
        for j in range(1, size):
            pl.semaphore_signal(
                barrier, inc=1, device_id={axis: lax.rem(me + j, size)}, device_id_type=MESH
            )

    def rank_list(flags):
        count = jnp.int32(0)
        out = []
        for flag in flags:
            out.append(flag * count + (1 - flag) * live)
            count = count + flag
        return out

    flags = [m_ref[t // tiles_c, t % tiles_c] for t in range(tiles)]
    for t in range(tiles):
        tr, tc = t // tiles_c, t % tiles_c
        by_tile[t] = v_ref[tr * EDGE : (tr + 1) * EDGE, tc * EDGE : (tc + 1) * EDGE]
    count = jnp.int32(0)
    upto = []
    for t in range(tiles):
        count = count + flags[t]
        upto.append(count)
    zero_tile = jnp.zeros((EDGE, EDGE), jnp.bfloat16)
    for s in range(live):
        index = jnp.int32(0)
        for t in range(tiles - 1):
            index = index + lax.select(upto[t] <= s, jnp.int32(1), jnp.int32(0))
        pack[s] = by_tile[index]
    pack[live] = zero_tile
    own_ranks = rank_list(flags)
    for t in range(tiles):
        ranks[t] = own_ranks[t]
    for buf in (*from_left, *from_right):
        buf[live] = zero_tile
    for t in range(tiles):
        mask_all[c, t // tiles_c, t % tiles_c] = flags[t]

    pl.semaphore_wait(barrier, n_col - 1 + n_row - 1 + n_layer - 1)

    sends = []

    def slots(layer, ch):
        return pl.ds(layer * part + ch * chunk, chunk)

    def z_copy(way, s, ch):
        bufs = from_left if way == 0 else from_right
        src = pack if s == 1 else bufs[s - 2]
        where = slots(l, ch)
        return pltpu.make_async_remote_copy(
            src_ref=src.at[where], dst_ref=bufs[s - 1].at[where],
            send_sem=z_send.at[way, s - 1, ch], recv_sem=z_recv.at[way, s - 1, ch],
            device_id={"col": c + 1 if way == 0 else c - 1}, device_id_type=MESH,
        )

    def y_copy(way, s, ch, j, layer):
        buf = (from_left if way == 0 else from_right)[s - 1]
        where = slots(layer, ch)
        return pltpu.make_async_remote_copy(
            src_ref=buf.at[where], dst_ref=buf.at[where],
            send_sem=y_send.at[way, s - 1, ch, j - 1], recv_sem=y_recv.at[way, s - 1, ch, j - 1],
            device_id={"layer": lax.rem(l + j, n_layer)}, device_id_type=MESH,
        )

    def here(way, s):
        return c >= s if way == 0 else c + s < n_col

    def sends_on(way, s):
        if way == 0:
            return (c + 1 < n_col) & (c >= s - 1)
        return (c >= 1) & (c + s - 1 < n_col)

    def z_start(s, ch):
        for way in (0, 1):
            @pl.when(sends_on(way, s))
            def _():
                z_copy(way, s, ch).start()

    for ch in range(CHUNKS):
        z_start(1, ch)

    def to_peers(axis, me, size, ref, send, recv):
        copies = []
        for j in range(1, size):
            copy = pltpu.make_async_remote_copy(
                src_ref=ref.at[me], dst_ref=ref.at[me],
                send_sem=send.at[j - 1], recv_sem=recv.at[j - 1],
                device_id={axis: lax.rem(me + j, size)}, device_id_type=MESH,
            )
            copy.start()
            sends.append(copy)
            copies.append(copy)
        return copies

    mask_copies = to_peers("col", c, n_col, mask_all, mask_send, mask_recv)

    for tc in range(tiles_c):
        total = jnp.zeros((EDGE, EDGE), jnp.float32)
        for tr in range(tiles_r):
            total = total + pack[own_ranks[tr * tiles_c + tc]].astype(jnp.float32)
        mpart[r, :, tc * EDGE : (tc + 1) * EDGE] = jnp.sum(total, axis=0, keepdims=True)
    mp_copies = to_peers("row", r, n_row, mpart, mp_send, mp_recv)

    for tr in range(tiles_r):
        for j in range(half_tiles):
            rank = ranks[tr * tiles_c + l * half_tiles + j]
            rbuf[r, tr * EDGE : (tr + 1) * EDGE, j * EDGE : (j + 1) * EDGE] = pack[rank]

    sibling = r + 1 - 2 * lax.rem(r, 2)
    pairs = n_row // 2

    def x_copy(k, section, target):
        return pltpu.make_async_remote_copy(
            src_ref=rbuf.at[section], dst_ref=rbuf.at[section],
            send_sem=x_send.at[k], recv_sem=x_recv.at[k],
            device_id={"row": target}, device_id_type=MESH,
        )

    across = [lax.rem(r + 2 * j, n_row) for j in range(1, pairs)]
    for j, target in enumerate(across):
        x_copy(1 + j, r, target).start()
    x_copy(0, r, sibling).start()

    for copy in mp_copies:
        copy.wait_recv()
    total = mpart[0]
    for j in range(1, n_row):
        total = total + mpart[j]
    mass[c] = total
    ms_copies = to_peers("col", c, n_col, mass, ms_send, ms_recv)

    def forward(s):
        for ch in range(CHUNKS):
            for way in (0, 1):
                @pl.when(here(way, s))
                def _():
                    z_copy(way, s, ch).wait_recv()
                    if s < steps:
                        @pl.when(sends_on(way, s + 1))
                        def _():
                            z_copy(way, s + 1, ch).start()
                    for j in range(1, n_layer):
                        y_copy(way, s, ch, j, l).start()

    def product(buf, block):
        scale = 1.0 / mass[block]
        flags = [mask_all[block, t // tiles_c, t % tiles_c] for t in range(tiles)]
        local = rank_list(flags)
        section, offset = block // per, (block % per) * width
        right = rbuf[section, pl.ds(pl.multiple_of(offset, EDGE), width), :]
        rows_at_once = min(tiles_r, 4)
        for first in range(0, tiles_r, rows_at_once):
            rows = []
            for tr in range(first, first + rows_at_once):
                row = []
                for tc in range(tiles_c):
                    tile = buf[local[tr * tiles_c + tc]].astype(jnp.float32)
                    row.append((tile * scale[:, tc * EDGE : (tc + 1) * EDGE]).astype(jnp.bfloat16))
                rows.append(jnp.concatenate(row, axis=1))
            left = jnp.concatenate(rows, axis=0)
            span = slice(first * EDGE, (first + rows_at_once) * EDGE)
            acc[span, :] += jnp.dot(left, right, preferred_element_type=jnp.float32)

    def foreign(s):
        for way in (0, 1):
            @pl.when(here(way, s))
            def _():
                for ch in range(CHUNKS):
                    for j in range(1, n_layer):
                        y_copy(way, s, ch, j, lax.rem(l + n_layer - j, n_layer)).wait_recv()
                product(
                    (from_left if way == 0 else from_right)[s - 1],
                    c - s if way == 0 else c + s,
                )

    acc[...] = jnp.zeros_like(acc)
    for s in range(1, max(steps, 2)):
        forward(s)
    for j, target in enumerate(across):
        x_copy(1 + j, lax.rem(r + n_row - 2 * (j + 1), n_row), target).wait_recv()
        x_copy(pairs + j, lax.rem(r + n_row - 2 * (j + 1), n_row), sibling).start()
    x_copy(0, sibling, sibling).wait_recv()
    for j in range(len(across)):
        x_copy(pairs + j, lax.rem(sibling + n_row - 2 * (j + 1), n_row), sibling).wait_recv()
    for copy in (*mask_copies, *ms_copies):
        copy.wait_recv()
    product(pack, c)
    for s in range(1, steps - 1):
        foreign(s)
    if steps >= 2:
        forward(steps)
    for s in range(max(steps - 1, 1), steps + 1):
        foreign(s)

    inflated = acc[...] * acc[...]
    infl_ref[...] = inflated
    wpart[r] = jnp.sum(inflated, axis=0, keepdims=True)
    for copy in to_peers("row", r, n_row, wpart, w_send, w_recv):
        copy.wait_recv()
    total = wpart[0]
    for j in range(1, n_row):
        total = total + wpart[j]
    scale_ref[...] = (height * n_row * 1.0) / total

    for copy in sends:
        copy.wait_send()
    for j, target in enumerate(across):
        x_copy(1 + j, r, target).wait_send()
        x_copy(pairs + j, r, sibling).wait_send()
    x_copy(0, r, sibling).wait_send()
    for s in range(1, steps + 1):
        for way in (0, 1):
            @pl.when(sends_on(way, s))
            def _():
                for ch in range(CHUNKS):
                    z_copy(way, s, ch).wait_send()

            @pl.when(here(way, s))
            def _():
                for ch in range(CHUNKS):
                    for j in range(1, n_layer):
                        y_copy(way, s, ch, j, l).wait_send()


def shards(values, tile_mask):
    n_row, n_col, n_layer = (lax.axis_size(a) for a in ("row", "col", "layer"))
    height, width = values.shape
    tiles_r, tiles_c = tile_mask.shape
    live = tiles_r * tiles_c // 2
    half = width // n_layer
    dims = (n_row, n_col, n_layer, tiles_r, tiles_c, live)
    steps = n_col - 1
    dma = pltpu.SemaphoreType.DMA
    inflated, scale = pl.pallas_call(
        functools.partial(kernel, dims),
        out_shape=(
            jax.ShapeDtypeStruct((height, half), jnp.float32),
            jax.ShapeDtypeStruct((1, half), jnp.float32),
        ),
        in_specs=[
            pl.BlockSpec(memory_space=pltpu.VMEM),
            pl.BlockSpec(memory_space=pltpu.SMEM),
        ],
        out_specs=(pl.BlockSpec(memory_space=pltpu.VMEM),) * 2,
        scratch_shapes=[
            pltpu.VMEM((tiles_r * tiles_c, EDGE, EDGE), jnp.bfloat16),
            pltpu.VMEM((live + 1, EDGE, EDGE), jnp.bfloat16),
            pltpu.VMEM((n_row, height, half), jnp.bfloat16),
            pltpu.VMEM((height, half), jnp.float32),
            pltpu.SMEM((n_col, tiles_r, tiles_c), jnp.int32),
            pltpu.SMEM((tiles_r * tiles_c,), jnp.int32),
            pltpu.VMEM((n_row, 1, width), jnp.float32),
            pltpu.VMEM((n_col, 1, width), jnp.float32),
            pltpu.VMEM((n_row, 1, half), jnp.float32),
            *[pltpu.VMEM((live + 1, EDGE, EDGE), jnp.bfloat16)] * (2 * steps),
            dma((2, steps, CHUNKS)),
            dma((2, steps, CHUNKS)),
            dma((2, steps, CHUNKS, n_layer - 1)),
            dma((2, steps, CHUNKS, n_layer - 1)),
            dma((n_row,)),
            dma((n_row,)),
            dma((n_col - 1,)),
            dma((n_col - 1,)),
            dma((n_row - 1,)),
            dma((n_row - 1,)),
            dma((n_col - 1,)),
            dma((n_col - 1,)),
            dma((n_row - 1,)),
            dma((n_row - 1,)),
        ],
        compiler_params=pltpu.CompilerParams(
            collective_id=0, has_side_effects=True, vmem_limit_bytes=56 * 2**20
        ),
        name="markov_step",
    )(values, tile_mask)
    return inflated * scale


def solution(mesh):
    return jax.shard_map(
        shards,
        mesh=mesh,
        in_specs=(P("row", "col"), P("row", "col")),
        out_specs=P("row", ("col", "layer")),
        check_vma=False,
    )
```

time: 149 us -> 29 us (0.19)
  waiting for transfers between devices: 112 us -> 0 us
  Pallas kernels: 0 us -> 26.2 us
  blocking collectives: 15.2 us -> 0 us
  between operations: 13.1 us -> 0.02 us
  other arithmetic: 5.22 us -> 1.87 us
  matrix products: 3.15 us -> 0 us
    psum x2 -> x0, waiting for transfers between devices: 91 us -> none  [broadcast(): return lax.psum(block, axis)]
    pallas_call x0 -> x1, Pallas kernels: none -> 26.2 us  [shards(): pl.pallas_call(functools.partial(kernel, dims), out_shape=(jax.ShapeDtype...]
    reduce_scatter x1 -> x0, waiting for transfers between devices: 19.9 us -> none  [shards(): expanded = lax.psum_scatter(total, 'layer', scatter_dimension=1, tiled=True)]
    psum x2 -> x0, blocking collectives: 15.2 us -> none  [the longest x1 8.33 us: shards(): mass = lax.psum(jnp.sum(masked, axis=0, dtype=jnp.float32), 'row')]
    dot_general x2 -> x0, matrix products: 3.15 us -> none  [shards(): total = total + jnp.dot(left, right, preferred_element_type=jnp.float32)]
    select_n x2 -> x0, other arithmetic: 2.25 us -> none  [broadcast(): jnp.where(lax.axis_index(axis) == source, block, jnp.zeros_like(block))]
    mul x0 -> x1, other arithmetic: none -> 1.87 us  [shards(): return inflated * scale]
  transfers between devices with their start and end apart: 3 -> 0, of which waited for: 3 -> 0; matrix products, arithmetic and copies ran while one was open for 0% -> 0% of each run, Pallas kernels for 0% -> 0%
where the time goes in v1:
time: 29 us; the launch traced here: 28.8 us
  Pallas kernels  26.2 us (90%)
  other arithmetic  1.87 us (6%)
  local copies, waits for them, and re-layouts  0.66 us (2%)
    pallas_call x1, Pallas kernels, shards(): pl.pallas_call(functools.partial(kernel, dims), out_shape=(jax.ShapeDtype...  26.2 us
    mul x1, other arithmetic, shards(): return inflated * scale  1.87 us
    unnamed x2, local copies, waits for them, and re-layouts  0.66 us

profile of v1, /device:TPU:0, one launch (start us, length us, event | category | flops | bytes accessed | tf_op | source)
XLA Modules:
  0.0 28.8 jit_solution(17605234756979430396)
XLA Ops:
  0.0 26.2 %markov_step.1 = (f32[512,256]{1,0:T(8,128)}, f32[1,256]{1,0:T(1,128)}) custom-call(bf16[512,512]{1,0:T(8,128)(2,1)} %v_ref.1, s32[4,4]{1,0:T(4,128)} %m_ref.1), custom_call_target="tpu_custom_call" | custom-call | tf_op jit(solution)/shard_map/markov_step/pallas_call | solution.py:270
  26.3 0.0 copy-start
  26.3 0.7 %copy-done = f32[1,256]{1,0:T(1,128)S(1)} copy-done((f32[1,256]{1,0:T(1,128)S(1)}, f32[1,256]{1,0:T(1,128)}, u32[]{:S(2)}) %copy-start) | copy-done | bytes 1048
  26.9 1.9 %broadcast_multiply_fusion = f32[512,256]{1,0:T(8,128)} fusion(f32[512,256]{1,0:T(8,128)} %get-tuple-element.7, f32[256]{0:T(256)S(1)} %bitcast.1), kind=kLoop, calls=%fused_computation | loop fusion | flops 131072 | bytes 1049600 | tf_op jit(solution)/shard_map/mul | solution.py:312
Async XLA Ops:
  26.3 0.7 %copy-start = (f32[1,256]{1,0:T(1,128)S(1)}, f32[1,256]{1,0:T(1,128)}, u32[]{:S(2)}) copy-start(f32[1,256]{1,0:T(1,128)} %get-tuple-element.8) | copy-start | bytes 3076

commit v2 on v1

--- a/solution.py
+++ b/solution.py
@@ -13,14 +13,14 @@
 
 
 def kernel(
-    dims, v_ref, m_ref, infl_ref, scale_ref,
+    dims, v_ref, m_ref, out_ref,
     by_tile, pack, rbuf, acc, mask_all, ranks, mpart, mass, wpart, *rest,
 ):
     n_row, n_col, n_layer, tiles_r, tiles_c, live = dims
     steps = n_col - 1
     from_left = rest[:steps]
     from_right = rest[steps : 2 * steps]
-    (z_send, z_recv, y_send, y_recv, x_send, x_recv, mask_send, mask_recv,
+    (in_sem, z_send, z_recv, y_send, y_recv, x_send, x_recv, mask_send, mask_recv,
      mp_send, mp_recv, ms_send, ms_recv, w_send, w_recv) = rest[2 * steps :]
     height, width = tiles_r * EDGE, tiles_c * EDGE
     half = width // n_layer
@@ -34,11 +34,33 @@
     l = lax.axis_index("layer")
 
     barrier = pltpu.get_barrier_semaphore()
-    for axis, me, size in (("col", c, n_col), ("row", r, n_row), ("layer", l, n_layer)):
+    for axis, me, size in (("row", r, n_row), ("layer", l, n_layer)):
         for j in range(1, size):
             pl.semaphore_signal(
                 barrier, inc=1, device_id={axis: lax.rem(me + j, size)}, device_id_type=MESH
             )
+
+    @pl.when(c > 0)
+    def _():
+        pl.semaphore_signal(barrier, inc=1, device_id={"col": c - 1}, device_id_type=MESH)
+
+    @pl.when(c + 1 < n_col)
+    def _():
+        pl.semaphore_signal(barrier, inc=1, device_id={"col": c + 1}, device_id_type=MESH)
+
+    mask_in = pltpu.make_async_copy(m_ref, mask_all.at[c], in_sem.at[0])
+    mask_in.start()
+    for t in range(tiles):
+        tr, tc = t // tiles_c, t % tiles_c
+        pltpu.make_async_copy(
+            v_ref.at[tr * EDGE : (tr + 1) * EDGE, tc * EDGE : (tc + 1) * EDGE],
+            by_tile.at[t], in_sem.at[1],
+        ).start()
+    zero_tile = jnp.zeros((EDGE, EDGE), jnp.bfloat16)
+    for buf in (pack, *from_left, *from_right):
+        buf[live] = zero_tile
+    acc[...] = jnp.zeros_like(acc)
+    mask_in.wait()
 
     def rank_list(flags):
         count = jnp.int32(0)
@@ -48,31 +70,35 @@
             count = count + flag
         return out
 
-    flags = [m_ref[t // tiles_c, t % tiles_c] for t in range(tiles)]
-    for t in range(tiles):
-        tr, tc = t // tiles_c, t % tiles_c
-        by_tile[t] = v_ref[tr * EDGE : (tr + 1) * EDGE, tc * EDGE : (tc + 1) * EDGE]
+    flags = [mask_all[c, t // tiles_c, t % tiles_c] for t in range(tiles)]
     count = jnp.int32(0)
     upto = []
     for t in range(tiles):
         count = count + flags[t]
         upto.append(count)
-    zero_tile = jnp.zeros((EDGE, EDGE), jnp.bfloat16)
+    pltpu.make_async_copy(by_tile, by_tile, in_sem.at[1]).wait()
     for s in range(live):
         index = jnp.int32(0)
         for t in range(tiles - 1):
             index = index + lax.select(upto[t] <= s, jnp.int32(1), jnp.int32(0))
         pack[s] = by_tile[index]
-    pack[live] = zero_tile
     own_ranks = rank_list(flags)
     for t in range(tiles):
         ranks[t] = own_ranks[t]
-    for buf in (*from_left, *from_right):
-        buf[live] = zero_tile
-    for t in range(tiles):
-        mask_all[c, t // tiles_c, t % tiles_c] = flags[t]
-
-    pl.semaphore_wait(barrier, n_col - 1 + n_row - 1 + n_layer - 1)
+
+    for tc in range(tiles_c):
+        total = jnp.zeros((EDGE, EDGE), jnp.float32)
+        for tr in range(tiles_r):
+            total = total + pack[own_ranks[tr * tiles_c + tc]].astype(jnp.float32)
+        mpart[r, :, tc * EDGE : (tc + 1) * EDGE] = jnp.sum(total, axis=0, keepdims=True)
+
+    for tr in range(tiles_r):
+        for j in range(half_tiles):
+            rank = ranks[tr * tiles_c + l * half_tiles + j]
+            rbuf[r, tr * EDGE : (tr + 1) * EDGE, j * EDGE : (j + 1) * EDGE] = pack[rank]
+
+    neighbours = lax.select(c > 0, 1, 0) + lax.select(c + 1 < n_col, 1, 0)
+    pl.semaphore_wait(barrier, n_row - 1 + n_layer - 1 + neighbours)
 
     sends = []
 
@@ -128,19 +154,29 @@
             copies.append(copy)
         return copies
 
-    mask_copies = to_peers("col", c, n_col, mask_all, mask_send, mask_recv)
-
-    for tc in range(tiles_c):
-        total = jnp.zeros((EDGE, EDGE), jnp.float32)
-        for tr in range(tiles_r):
-            total = total + pack[own_ranks[tr * tiles_c + tc]].astype(jnp.float32)
-        mpart[r, :, tc * EDGE : (tc + 1) * EDGE] = jnp.sum(total, axis=0, keepdims=True)
+    def hand_on(ref, send, recv, way, s):
+        block = c - (s - 1) if way == 0 else c + (s - 1)
+        return pltpu.make_async_remote_copy(
+            src_ref=ref.at[block], dst_ref=ref.at[block],
+            send_sem=send.at[way, s - 1], recv_sem=recv.at[way, s - 1],
+            device_id={"col": c + 1 if way == 0 else c - 1}, device_id_type=MESH,
+        )
+
+    def received(ref, send, recv, way, s):
+        block = c - s if way == 0 else c + s
+        return pltpu.make_async_remote_copy(
+            src_ref=ref.at[block], dst_ref=ref.at[block],
+            send_sem=send.at[way, s - 1], recv_sem=recv.at[way, s - 1],
+            device_id={"col": c + 1 if way == 0 else c - 1}, device_id_type=MESH,
+        )
+
+    small = ((mask_all, mask_send, mask_recv), (mass, ms_send, ms_recv))
+
     mp_copies = to_peers("row", r, n_row, mpart, mp_send, mp_recv)
-
-    for tr in range(tiles_r):
-        for j in range(half_tiles):
-            rank = ranks[tr * tiles_c + l * half_tiles + j]
-            rbuf[r, tr * EDGE : (tr + 1) * EDGE, j * EDGE : (j + 1) * EDGE] = pack[rank]
+    for way in (0, 1):
+        @pl.when(sends_on(way, 1))
+        def _():
+            hand_on(*small[0], way, 1).start()
 
     sibling = r + 1 - 2 * lax.rem(r, 2)
     pairs = n_row // 2
@@ -163,7 +199,10 @@
     for j in range(1, n_row):
         total = total + mpart[j]
     mass[c] = total
-    ms_copies = to_peers("col", c, n_col, mass, ms_send, ms_recv)
+    for way in (0, 1):
+        @pl.when(sends_on(way, 1))
+        def _():
+            hand_on(*small[1], way, 1).start()
 
     def forward(s):
         for ch in range(CHUNKS):
@@ -177,6 +216,16 @@
                             z_copy(way, s + 1, ch).start()
                     for j in range(1, n_layer):
                         y_copy(way, s, ch, j, l).start()
+        for way in (0, 1):
+            @pl.when(here(way, s))
+            def _():
+                for group in small:
+                    received(*group, way, s).wait_recv()
+                if s < steps:
+                    @pl.when(sends_on(way, s + 1))
+                    def _():
+                        for group in small:
+                            hand_on(*group, way, s + 1).start()
 
     def product(buf, block):
         scale = 1.0 / mass[block]
@@ -209,7 +258,6 @@
                     c - s if way == 0 else c + s,
                 )
 
-    acc[...] = jnp.zeros_like(acc)
     for s in range(1, max(steps, 2)):
         forward(s)
     for j, target in enumerate(across):
@@ -218,8 +266,6 @@
     x_copy(0, sibling, sibling).wait_recv()
     for j in range(len(across)):
         x_copy(pairs + j, lax.rem(sibling + n_row - 2 * (j + 1), n_row), sibling).wait_recv()
-    for copy in (*mask_copies, *ms_copies):
-        copy.wait_recv()
     product(pack, c)
     for s in range(1, steps - 1):
         foreign(s)
@@ -229,14 +275,14 @@
         foreign(s)
 
     inflated = acc[...] * acc[...]
-    infl_ref[...] = inflated
+    acc[...] = inflated
     wpart[r] = jnp.sum(inflated, axis=0, keepdims=True)
     for copy in to_peers("row", r, n_row, wpart, w_send, w_recv):
         copy.wait_recv()
     total = wpart[0]
     for j in range(1, n_row):
         total = total + wpart[j]
-    scale_ref[...] = (height * n_row * 1.0) / total
+    out_ref[...] = acc[...] * ((height * n_row * 1.0) / total)
 
     for copy in sends:
         copy.wait_send()
@@ -250,6 +296,8 @@
             def _():
                 for ch in range(CHUNKS):
                     z_copy(way, s, ch).wait_send()
+                for group in small:
+                    hand_on(*group, way, s).wait_send()
 
             @pl.when(here(way, s))
             def _():
@@ -267,17 +315,11 @@
     dims = (n_row, n_col, n_layer, tiles_r, tiles_c, live)
     steps = n_col - 1
     dma = pltpu.SemaphoreType.DMA
-    inflated, scale = pl.pallas_call(
+    return pl.pallas_call(
         functools.partial(kernel, dims),
-        out_shape=(
-            jax.ShapeDtypeStruct((height, half), jnp.float32),
-            jax.ShapeDtypeStruct((1, half), jnp.float32),
-        ),
-        in_specs=[
-            pl.BlockSpec(memory_space=pltpu.VMEM),
-            pl.BlockSpec(memory_space=pltpu.SMEM),
-        ],
-        out_specs=(pl.BlockSpec(memory_space=pltpu.VMEM),) * 2,
+        out_shape=jax.ShapeDtypeStruct((height, half), jnp.float32),
+        in_specs=[pl.BlockSpec(memory_space=pl.ANY)] * 2,
+        out_specs=pl.BlockSpec(memory_space=pltpu.VMEM),
         scratch_shapes=[
             pltpu.VMEM((tiles_r * tiles_c, EDGE, EDGE), jnp.bfloat16),
             pltpu.VMEM((live + 1, EDGE, EDGE), jnp.bfloat16),
@@ -289,18 +331,19 @@
             pltpu.VMEM((n_col, 1, width), jnp.float32),
             pltpu.VMEM((n_row, 1, half), jnp.float32),
             *[pltpu.VMEM((live + 1, EDGE, EDGE), jnp.bfloat16)] * (2 * steps),
+            dma((2,)),
             dma((2, steps, CHUNKS)),
             dma((2, steps, CHUNKS)),
             dma((2, steps, CHUNKS, n_layer - 1)),
             dma((2, steps, CHUNKS, n_layer - 1)),
             dma((n_row,)),
             dma((n_row,)),
-            dma((n_col - 1,)),
-            dma((n_col - 1,)),
+            dma((2, steps)),
+            dma((2, steps)),
             dma((n_row - 1,)),
             dma((n_row - 1,)),
-            dma((n_col - 1,)),
-            dma((n_col - 1,)),
+            dma((2, steps)),
+            dma((2, steps)),
             dma((n_row - 1,)),
             dma((n_row - 1,)),
         ],
@@ -309,7 +352,6 @@
         ),
         name="markov_step",
     )(values, tile_mask)
-    return inflated * scale
 
 
 def solution(mesh):

time: 29 us -> 27 us (0.931)
  other arithmetic: 1.87 us -> 0 us
  Pallas kernels: 26.2 us -> 24.8 us
  local copies, waits for them, and re-layouts: 0.66 us -> 1.87 us
    mul x1 -> x0, other arithmetic: 1.87 us -> none  [shards(): return inflated * scale]
    pallas_call x1, Pallas kernels: 26.2 us -> 24.8 us  [shards(): pl.pallas_call(functools.partial(kernel, dims), out_shape=jax.ShapeDtypeS...]
    unnamed x2 -> x1, local copies, waits for them, and re-layouts: 0.66 us -> 1.87 us
where the time goes in v2:
time: 27 us; the launch traced here: 26.7 us
  Pallas kernels  24.8 us (92%)
  local copies, waits for them, and re-layouts  1.87 us (7%)
    pallas_call x1, Pallas kernels, shards(): pl.pallas_call(functools.partial(kernel, dims), out_shape=jax.ShapeDtypeS...  24.8 us
    unnamed x1, local copies, waits for them, and re-layouts  1.87 us

profile of v2, /device:TPU:0, one launch (start us, length us, event | category | flops | bytes accessed | tf_op | source)
XLA Modules:
  0.0 26.7 jit_solution(12526253273482361495)
XLA Ops:
  0.0 24.8 %markov_step.1 = f32[512,256]{1,0:T(8,128)} custom-call(bf16[512,512]{1,0:T(8,128)(2,1)} %v_ref.1, s32[4,4]{1,0:T(4,128)} %m_ref.1), custom_call_target="tpu_custom_call" | custom-call | tf_op jit(solution)/shard_map/markov_step/pallas_call | solution.py:318
  24.8 1.9 %copy.4 = f32[512,256]{1,0:T(8,128)} copy(f32[512,256]{1,0:T(8,128)} %markov_step.1) | data formatting | bytes 1048576

commit v3 on v2

--- a/solution.py
+++ b/solution.py
@@ -9,7 +9,7 @@
 
 MESH = pl.DeviceIdType.MESH
 EDGE = 128
-CHUNKS = 2
+CHUNKS = 4
 
 
 def kernel(

time: 27 us -> 27 us (level)
  no operation moved by 1% of the time
where the time goes in v3:
time: 27 us; the launch traced here: 26.8 us
  Pallas kernels  24.9 us (92%)
  local copies, waits for them, and re-layouts  1.87 us (7%)
    pallas_call x1, Pallas kernels, shards(): pl.pallas_call(functools.partial(kernel, dims), out_shape=jax.ShapeDtypeS...  24.9 us
    unnamed x1, local copies, waits for them, and re-layouts  1.87 us

profile of v3, /device:TPU:0, one launch (start us, length us, event | category | flops | bytes accessed | tf_op | source)
XLA Modules:
  0.0 26.8 jit_solution(13058237651583855334)
XLA Ops:
  0.0 24.9 %markov_step.1 = f32[512,256]{1,0:T(8,128)} custom-call(bf16[512,512]{1,0:T(8,128)(2,1)} %v_ref.1, s32[4,4]{1,0:T(4,128)} %m_ref.1), custom_call_target="tpu_custom_call" | custom-call | tf_op jit(solution)/shard_map/markov_step/pallas_call | solution.py:318
  24.9 1.9 %copy.4 = f32[512,256]{1,0:T(8,128)} copy(f32[512,256]{1,0:T(8,128)} %markov_step.1) | data formatting | bytes 1048576

commit v4 on v2

--- a/solution.py
+++ b/solution.py
@@ -13,15 +13,15 @@
 
 
 def kernel(
-    dims, v_ref, m_ref, out_ref,
-    by_tile, pack, rbuf, acc, mask_all, ranks, mpart, mass, wpart, *rest,
+    dims, v_ref, m_ref, acc, scale_ref,
+    by_tile, pack, rbuf, left, mask, ranks, mpart, mass, wpart, *rest,
 ):
     n_row, n_col, n_layer, tiles_r, tiles_c, live = dims
     steps = n_col - 1
     from_left = rest[:steps]
-    from_right = rest[steps : 2 * steps]
-    (in_sem, z_send, z_recv, y_send, y_recv, x_send, x_recv, mask_send, mask_recv,
-     mp_send, mp_recv, ms_send, ms_recv, w_send, w_recv) = rest[2 * steps :]
+    from_right = from_left[::-1]
+    (in_sem, z_send, z_recv, y_send, y_recv, x_send, x_recv, rank_send, rank_recv,
+     mp_send, mp_recv, ms_send, ms_recv, w_send, w_recv) = rest[steps:]
     height, width = tiles_r * EDGE, tiles_c * EDGE
     half = width // n_layer
     half_tiles = tiles_c // n_layer
@@ -48,7 +48,7 @@
     def _():
         pl.semaphore_signal(barrier, inc=1, device_id={"col": c + 1}, device_id_type=MESH)
 
-    mask_in = pltpu.make_async_copy(m_ref, mask_all.at[c], in_sem.at[0])
+    mask_in = pltpu.make_async_copy(m_ref, mask, in_sem.at[0])
     mask_in.start()
     for t in range(tiles):
         tr, tc = t // tiles_c, t % tiles_c
@@ -57,7 +57,7 @@
             by_tile.at[t], in_sem.at[1],
         ).start()
     zero_tile = jnp.zeros((EDGE, EDGE), jnp.bfloat16)
-    for buf in (pack, *from_left, *from_right):
+    for buf in (pack, *from_left):
         buf[live] = zero_tile
     acc[...] = jnp.zeros_like(acc)
     mask_in.wait()
@@ -70,7 +70,7 @@
             count = count + flag
         return out
 
-    flags = [mask_all[c, t // tiles_c, t % tiles_c] for t in range(tiles)]
+    flags = [mask[t // tiles_c, t % tiles_c] for t in range(tiles)]
     count = jnp.int32(0)
     upto = []
     for t in range(tiles):
@@ -84,7 +84,7 @@
         pack[s] = by_tile[index]
     own_ranks = rank_list(flags)
     for t in range(tiles):
-        ranks[t] = own_ranks[t]
+        ranks[c, t // tiles_c, t % tiles_c] = own_ranks[t]
 
     for tc in range(tiles_c):
         total = jnp.zeros((EDGE, EDGE), jnp.float32)
@@ -94,7 +94,7 @@
 
     for tr in range(tiles_r):
         for j in range(half_tiles):
-            rank = ranks[tr * tiles_c + l * half_tiles + j]
+            rank = ranks[c, tr, l * half_tiles + j]
             rbuf[r, tr * EDGE : (tr + 1) * EDGE, j * EDGE : (j + 1) * EDGE] = pack[rank]
 
     neighbours = lax.select(c > 0, 1, 0) + lax.select(c + 1 < n_col, 1, 0)
@@ -170,7 +170,7 @@
             device_id={"col": c + 1 if way == 0 else c - 1}, device_id_type=MESH,
         )
 
-    small = ((mask_all, mask_send, mask_recv), (mass, ms_send, ms_recv))
+    small = ((ranks, rank_send, rank_recv), (mass, ms_send, ms_recv))
 
     mp_copies = to_peers("row", r, n_row, mpart, mp_send, mp_recv)
     for way in (0, 1):
@@ -227,24 +227,18 @@
                         for group in small:
                             hand_on(*group, way, s + 1).start()
 
-    def product(buf, block):
+    def unpack(buf, block):
         scale = 1.0 / mass[block]
-        flags = [mask_all[block, t // tiles_c, t % tiles_c] for t in range(tiles)]
-        local = rank_list(flags)
-        section, offset = block // per, (block % per) * width
-        right = rbuf[section, pl.ds(pl.multiple_of(offset, EDGE), width), :]
-        rows_at_once = min(tiles_r, 4)
-        for first in range(0, tiles_r, rows_at_once):
-            rows = []
-            for tr in range(first, first + rows_at_once):
-                row = []
-                for tc in range(tiles_c):
-                    tile = buf[local[tr * tiles_c + tc]].astype(jnp.float32)
-                    row.append((tile * scale[:, tc * EDGE : (tc + 1) * EDGE]).astype(jnp.bfloat16))
-                rows.append(jnp.concatenate(row, axis=1))
-            left = jnp.concatenate(rows, axis=0)
-            span = slice(first * EDGE, (first + rows_at_once) * EDGE)
-            acc[span, :] += jnp.dot(left, right, preferred_element_type=jnp.float32)
+
+        def tile_row(tr, carry):
+            rows = pl.ds(pl.multiple_of(tr * EDGE, EDGE), EDGE)
+            for tc in range(tiles_c):
+                cols = slice(tc * EDGE, (tc + 1) * EDGE)
+                tile = buf[ranks[block, tr, tc]].astype(jnp.float32)
+                left[block, rows, cols] = (tile * scale[:, cols]).astype(jnp.bfloat16)
+            return carry
+
+        lax.fori_loop(0, tiles_r, tile_row, 0)
 
     def foreign(s):
         for way in (0, 1):
@@ -253,10 +247,34 @@
                 for ch in range(CHUNKS):
                     for j in range(1, n_layer):
                         y_copy(way, s, ch, j, lax.rem(l + n_layer - j, n_layer)).wait_recv()
-                product(
+                unpack(
                     (from_left if way == 0 else from_right)[s - 1],
                     c - s if way == 0 else c + s,
                 )
+
+    chunk_rows = min(height, 512)
+
+    def products(near, far):
+        def one(block, carry):
+            distance = jnp.abs(block - c)
+
+            @pl.when((distance >= near) & (distance < far))
+            def _():
+                section, offset = block // per, (block % per) * width
+                right = rbuf[section, pl.ds(pl.multiple_of(offset, EDGE), width), :]
+
+                def rows(i, inner):
+                    span = pl.ds(pl.multiple_of(i * chunk_rows, EDGE), chunk_rows)
+                    acc[span, :] += jnp.dot(
+                        left[block, span, :], right, preferred_element_type=jnp.float32
+                    )
+                    return inner
+
+                lax.fori_loop(0, height // chunk_rows, rows, 0)
+
+            return carry
+
+        lax.fori_loop(0, n_col, one, 0)
 
     for s in range(1, max(steps, 2)):
         forward(s)
@@ -266,13 +284,15 @@
     x_copy(0, sibling, sibling).wait_recv()
     for j in range(len(across)):
         x_copy(pairs + j, lax.rem(sibling + n_row - 2 * (j + 1), n_row), sibling).wait_recv()
-    product(pack, c)
+    unpack(pack, c)
     for s in range(1, steps - 1):
         foreign(s)
+    products(0, max(steps - 1, 1))
     if steps >= 2:
         forward(steps)
     for s in range(max(steps - 1, 1), steps + 1):
         foreign(s)
+    products(max(steps - 1, 1), n_col)
 
     inflated = acc[...] * acc[...]
     acc[...] = inflated
@@ -282,7 +302,7 @@
     total = wpart[0]
     for j in range(1, n_row):
         total = total + wpart[j]
-    out_ref[...] = acc[...] * ((height * n_row * 1.0) / total)
+    scale_ref[...] = (height * n_row * 1.0) / total
 
     for copy in sends:
         copy.wait_send()
@@ -306,6 +326,10 @@
                         y_copy(way, s, ch, j, l).wait_send()
 
 
+def scaled(inflated_ref, scale_ref, out_ref):
+    out_ref[...] = inflated_ref[...] * scale_ref[...]
+
+
 def shards(values, tile_mask):
     n_row, n_col, n_layer = (lax.axis_size(a) for a in ("row", "col", "layer"))
     height, width = values.shape
@@ -315,22 +339,25 @@
     dims = (n_row, n_col, n_layer, tiles_r, tiles_c, live)
     steps = n_col - 1
     dma = pltpu.SemaphoreType.DMA
-    return pl.pallas_call(
+    inflated, scale = pl.pallas_call(
         functools.partial(kernel, dims),
-        out_shape=jax.ShapeDtypeStruct((height, half), jnp.float32),
+        out_shape=(
+            pltpu.VMEM((height, half), jnp.float32),
+            pltpu.VMEM((1, half), jnp.float32),
+        ),
         in_specs=[pl.BlockSpec(memory_space=pl.ANY)] * 2,
-        out_specs=pl.BlockSpec(memory_space=pltpu.VMEM),
+        out_specs=(pl.BlockSpec(memory_space=pltpu.VMEM),) * 2,
         scratch_shapes=[
             pltpu.VMEM((tiles_r * tiles_c, EDGE, EDGE), jnp.bfloat16),
             pltpu.VMEM((live + 1, EDGE, EDGE), jnp.bfloat16),
             pltpu.VMEM((n_row, height, half), jnp.bfloat16),
-            pltpu.VMEM((height, half), jnp.float32),
+            pltpu.VMEM((n_col, height, width), jnp.bfloat16),
+            pltpu.SMEM((tiles_r, tiles_c), jnp.int32),
             pltpu.SMEM((n_col, tiles_r, tiles_c), jnp.int32),
-            pltpu.SMEM((tiles_r * tiles_c,), jnp.int32),
             pltpu.VMEM((n_row, 1, width), jnp.float32),
             pltpu.VMEM((n_col, 1, width), jnp.float32),
             pltpu.VMEM((n_row, 1, half), jnp.float32),
-            *[pltpu.VMEM((live + 1, EDGE, EDGE), jnp.bfloat16)] * (2 * steps),
+            *[pltpu.VMEM((live + 1, EDGE, EDGE), jnp.bfloat16)] * steps,
             dma((2,)),
             dma((2, steps, CHUNKS)),
             dma((2, steps, CHUNKS)),
@@ -352,6 +379,14 @@
         ),
         name="markov_step",
     )(values, tile_mask)
+    return pl.pallas_call(
+        scaled,
+        out_shape=jax.ShapeDtypeStruct((height, half), jnp.float32),
+        in_specs=[pl.BlockSpec(memory_space=pltpu.VMEM)] * 2,
+        out_specs=pl.BlockSpec(memory_space=pltpu.VMEM),
+        compiler_params=pltpu.CompilerParams(vmem_limit_bytes=8 * 2**20),
+        name="scaled",
+    )(inflated, scale)
 
 
 def solution(mesh):

time: 27 us -> 25.8 us (0.956)
  local copies, waits for them, and re-layouts: 1.87 us -> 0 us
  Pallas kernels: 24.8 us -> 25.6 us
    unnamed x1 -> x0, local copies, waits for them, and re-layouts: 1.87 us -> none
    pallas_call x1 -> x2, Pallas kernels: 24.8 us -> 25.6 us  [the longest x1 24.8 us: shards(): pl.pallas_call(functools.partial(kernel, dims), out_shape=(pltpu.VMEM((he...]
where the time goes in v4:
time: 25.8 us; the launch traced here: 25.6 us
  Pallas kernels  25.6 us (99%)
    pallas_call x1, Pallas kernels, shards(): pl.pallas_call(functools.partial(kernel, dims), out_shape=(pltpu.VMEM((he...  24.8 us
    pallas_call x1, Pallas kernels, shards(): pl.pallas_call(scaled, out_shape=jax.ShapeDtypeStruct((height, half), jnp...  0.83 us

profile of v4, /device:TPU:0, one launch (start us, length us, event | category | flops | bytes accessed | tf_op | source)
XLA Modules:
  0.0 25.6 jit_solution(3063096089067762366)
XLA Ops:
  0.0 24.8 %markov_step.1 = (f32[512,256]{1,0:T(8,128)S(1)}, f32[1,256]{1,0:T(1,128)S(1)}) custom-call(bf16[512,512]{1,0:T(8,128)(2,1)} %v_ref.1, s32[4,4]{1,0:T(4,128)} %m_ref.1), custom_call_target="tpu_custom_call" | custom-call | tf_op jit(solution)/shard_map/markov_step/pallas_call | solution.py:342
  24.8 0.8 %scaled.1 = f32[512,256]{1,0:T(8,128)} custom-call(f32[512,256]{1,0:T(8,128)S(1)} %get-tuple-element.7.inflated_ref, f32[1,256]{1,0:T(1,128)S(1)} %get-tuple-element.8.scale_ref), custom_call_target="tpu_custom_call" | custom-call | tf_op jit(solution)/shard_map/scaled/pallas_call | solution.py:382

commit v5 on v4

--- a/solution.py
+++ b/solution.py
@@ -86,17 +86,6 @@
     for t in range(tiles):
         ranks[c, t // tiles_c, t % tiles_c] = own_ranks[t]
 
-    for tc in range(tiles_c):
-        total = jnp.zeros((EDGE, EDGE), jnp.float32)
-        for tr in range(tiles_r):
-            total = total + pack[own_ranks[tr * tiles_c + tc]].astype(jnp.float32)
-        mpart[r, :, tc * EDGE : (tc + 1) * EDGE] = jnp.sum(total, axis=0, keepdims=True)
-
-    for tr in range(tiles_r):
-        for j in range(half_tiles):
-            rank = ranks[c, tr, l * half_tiles + j]
-            rbuf[r, tr * EDGE : (tr + 1) * EDGE, j * EDGE : (j + 1) * EDGE] = pack[rank]
-
     neighbours = lax.select(c > 0, 1, 0) + lax.select(c + 1 < n_col, 1, 0)
     pl.semaphore_wait(barrier, n_row - 1 + n_layer - 1 + neighbours)
 
@@ -138,8 +127,7 @@
             def _():
                 z_copy(way, s, ch).start()
 
-    for ch in range(CHUNKS):
-        z_start(1, ch)
+    z_start(1, 0)
 
     def to_peers(axis, me, size, ref, send, recv):
         copies = []
@@ -172,11 +160,23 @@
 
     small = ((ranks, rank_send, rank_recv), (mass, ms_send, ms_recv))
 
-    mp_copies = to_peers("row", r, n_row, mpart, mp_send, mp_recv)
     for way in (0, 1):
         @pl.when(sends_on(way, 1))
         def _():
             hand_on(*small[0], way, 1).start()
+
+    for tc in range(tiles_c):
+        total = jnp.zeros((EDGE, EDGE), jnp.float32)
+        for tr in range(tiles_r):
+            total = total + pack[own_ranks[tr * tiles_c + tc]].astype(jnp.float32)
+        mpart[r, :, tc * EDGE : (tc + 1) * EDGE] = jnp.sum(total, axis=0, keepdims=True)
+
+    mp_copies = to_peers("row", r, n_row, mpart, mp_send, mp_recv)
+
+    for tr in range(tiles_r):
+        for j in range(half_tiles):
+            rank = ranks[c, tr, l * half_tiles + j]
+            rbuf[r, tr * EDGE : (tr + 1) * EDGE, j * EDGE : (j + 1) * EDGE] = pack[rank]
 
     sibling = r + 1 - 2 * lax.rem(r, 2)
     pairs = n_row // 2
@@ -192,6 +192,13 @@
     for j, target in enumerate(across):
         x_copy(1 + j, r, target).start()
     x_copy(0, r, sibling).start()
+
+    for ch in range(1, CHUNKS):
+        for way in (0, 1):
+            @pl.when(sends_on(way, 1))
+            def _():
+                z_copy(way, 1, ch - 1).wait_send()
+                z_copy(way, 1, ch).start()
 
     for copy in mp_copies:
         copy.wait_recv()
@@ -216,6 +223,8 @@
                             z_copy(way, s + 1, ch).start()
                     for j in range(1, n_layer):
                         y_copy(way, s, ch, j, l).start()
+
+    def forward_small(s):
         for way in (0, 1):
             @pl.when(here(way, s))
             def _():
@@ -278,6 +287,9 @@
 
     for s in range(1, max(steps, 2)):
         forward(s)
+        if s > 1:
+            forward_small(s - 1)
+    forward_small(max(steps - 1, 1))
     for j, target in enumerate(across):
         x_copy(1 + j, lax.rem(r + n_row - 2 * (j + 1), n_row), target).wait_recv()
         x_copy(pairs + j, lax.rem(r + n_row - 2 * (j + 1), n_row), sibling).start()
@@ -290,6 +302,7 @@
     products(0, max(steps - 1, 1))
     if steps >= 2:
         forward(steps)
+        forward_small(steps)
     for s in range(max(steps - 1, 1), steps + 1):
         foreign(s)
     products(max(steps - 1, 1), n_col)
@@ -314,7 +327,7 @@
         for way in (0, 1):
             @pl.when(sends_on(way, s))
             def _():
-                for ch in range(CHUNKS):
+                for ch in range(CHUNKS - 1 if s == 1 else 0, CHUNKS):
                     z_copy(way, s, ch).wait_send()
                 for group in small:
                     hand_on(*group, way, s).wait_send()

time: 25.8 us -> 28.4 us (1.10)
  Pallas kernels: 25.6 us -> 28.2 us
    pallas_call x1, Pallas kernels: 24.8 us -> 27.3 us  [shards(): pl.pallas_call(functools.partial(kernel, dims), out_shape=(pltpu.VMEM((he...]
where the time goes in v5:
time: 28.4 us; the launch traced here: 28.2 us
  Pallas kernels  28.2 us (99%)
    pallas_call x1, Pallas kernels, shards(): pl.pallas_call(functools.partial(kernel, dims), out_shape=(pltpu.VMEM((he...  27.3 us
    pallas_call x1, Pallas kernels, shards(): pl.pallas_call(scaled, out_shape=jax.ShapeDtypeStruct((height, half), jnp...  0.83 us

profile of v5, /device:TPU:0, one launch (start us, length us, event | category | flops | bytes accessed | tf_op | source)
XLA Modules:
  0.0 28.2 jit_solution(13183007363470286206)
XLA Ops:
  0.0 27.3 %markov_step.1 = (f32[512,256]{1,0:T(8,128)S(1)}, f32[1,256]{1,0:T(1,128)S(1)}) custom-call(bf16[512,512]{1,0:T(8,128)(2,1)} %v_ref.1, s32[4,4]{1,0:T(4,128)} %m_ref.1), custom_call_target="tpu_custom_call" | custom-call | tf_op jit(solution)/shard_map/markov_step/pallas_call | solution.py:355
  27.3 0.8 %scaled.1 = f32[512,256]{1,0:T(8,128)} custom-call(f32[512,256]{1,0:T(8,128)S(1)} %get-tuple-element.7.inflated_ref, f32[1,256]{1,0:T(1,128)S(1)} %get-tuple-element.8.scale_ref), custom_call_target="tpu_custom_call" | custom-call | tf_op jit(solution)/shard_map/scaled/pallas_call | solution.py:395

commit v6 on v5

--- a/solution.py
+++ b/solution.py
@@ -34,19 +34,11 @@
     l = lax.axis_index("layer")
 
     barrier = pltpu.get_barrier_semaphore()
-    for axis, me, size in (("row", r, n_row), ("layer", l, n_layer)):
+    for axis, me, size in (("col", c, n_col), ("row", r, n_row), ("layer", l, n_layer)):
         for j in range(1, size):
             pl.semaphore_signal(
                 barrier, inc=1, device_id={axis: lax.rem(me + j, size)}, device_id_type=MESH
             )
-
-    @pl.when(c > 0)
-    def _():
-        pl.semaphore_signal(barrier, inc=1, device_id={"col": c - 1}, device_id_type=MESH)
-
-    @pl.when(c + 1 < n_col)
-    def _():
-        pl.semaphore_signal(barrier, inc=1, device_id={"col": c + 1}, device_id_type=MESH)
 
     mask_in = pltpu.make_async_copy(m_ref, mask, in_sem.at[0])
     mask_in.start()
@@ -86,8 +78,7 @@
     for t in range(tiles):
         ranks[c, t // tiles_c, t % tiles_c] = own_ranks[t]
 
-    neighbours = lax.select(c > 0, 1, 0) + lax.select(c + 1 < n_col, 1, 0)
-    pl.semaphore_wait(barrier, n_row - 1 + n_layer - 1 + neighbours)
+    pl.semaphore_wait(barrier, n_col - 1 + n_row - 1 + n_layer - 1)
 
     sends = []
 
@@ -96,12 +87,11 @@
 
     def z_copy(way, s, ch):
         bufs = from_left if way == 0 else from_right
-        src = pack if s == 1 else bufs[s - 2]
         where = slots(l, ch)
         return pltpu.make_async_remote_copy(
-            src_ref=src.at[where], dst_ref=bufs[s - 1].at[where],
+            src_ref=pack.at[where], dst_ref=bufs[s - 1].at[where],
             send_sem=z_send.at[way, s - 1, ch], recv_sem=z_recv.at[way, s - 1, ch],
-            device_id={"col": c + 1 if way == 0 else c - 1}, device_id_type=MESH,
+            device_id={"col": c + s if way == 0 else c - s}, device_id_type=MESH,
         )
 
     def y_copy(way, s, ch, j, layer):
@@ -117,17 +107,14 @@
         return c >= s if way == 0 else c + s < n_col
 
     def sends_on(way, s):
-        if way == 0:
-            return (c + 1 < n_col) & (c >= s - 1)
-        return (c >= 1) & (c + s - 1 < n_col)
-
-    def z_start(s, ch):
+        return c + s < n_col if way == 0 else c >= s
+
+    for s in range(steps, 0, -1):
         for way in (0, 1):
             @pl.when(sends_on(way, s))
             def _():
-                z_copy(way, s, ch).start()
-
-    z_start(1, 0)
+                for ch in range(CHUNKS):
+                    z_copy(way, s, ch).start()
 
     def to_peers(axis, me, size, ref, send, recv):
         copies = []
@@ -142,28 +129,7 @@
             copies.append(copy)
         return copies
 
-    def hand_on(ref, send, recv, way, s):
-        block = c - (s - 1) if way == 0 else c + (s - 1)
-        return pltpu.make_async_remote_copy(
-            src_ref=ref.at[block], dst_ref=ref.at[block],
-            send_sem=send.at[way, s - 1], recv_sem=recv.at[way, s - 1],
-            device_id={"col": c + 1 if way == 0 else c - 1}, device_id_type=MESH,
-        )
-
-    def received(ref, send, recv, way, s):
-        block = c - s if way == 0 else c + s
-        return pltpu.make_async_remote_copy(
-            src_ref=ref.at[block], dst_ref=ref.at[block],
-            send_sem=send.at[way, s - 1], recv_sem=recv.at[way, s - 1],
-            device_id={"col": c + 1 if way == 0 else c - 1}, device_id_type=MESH,
-        )
-
-    small = ((ranks, rank_send, rank_recv), (mass, ms_send, ms_recv))
-
-    for way in (0, 1):
-        @pl.when(sends_on(way, 1))
-        def _():
-            hand_on(*small[0], way, 1).start()
+    rank_copies = to_peers("col", c, n_col, ranks, rank_send, rank_recv)
 
     for tc in range(tiles_c):
         total = jnp.zeros((EDGE, EDGE), jnp.float32)
@@ -193,23 +159,13 @@
         x_copy(1 + j, r, target).start()
     x_copy(0, r, sibling).start()
 
-    for ch in range(1, CHUNKS):
-        for way in (0, 1):
-            @pl.when(sends_on(way, 1))
-            def _():
-                z_copy(way, 1, ch - 1).wait_send()
-                z_copy(way, 1, ch).start()
-
     for copy in mp_copies:
         copy.wait_recv()
     total = mpart[0]
     for j in range(1, n_row):
         total = total + mpart[j]
     mass[c] = total
-    for way in (0, 1):
-        @pl.when(sends_on(way, 1))
-        def _():
-            hand_on(*small[1], way, 1).start()
+    ms_copies = to_peers("col", c, n_col, mass, ms_send, ms_recv)
 
     def forward(s):
         for ch in range(CHUNKS):
@@ -217,25 +173,8 @@
                 @pl.when(here(way, s))
                 def _():
                     z_copy(way, s, ch).wait_recv()
-                    if s < steps:
-                        @pl.when(sends_on(way, s + 1))
-                        def _():
-                            z_copy(way, s + 1, ch).start()
                     for j in range(1, n_layer):
                         y_copy(way, s, ch, j, l).start()
-
-    def forward_small(s):
-        for way in (0, 1):
-            @pl.when(here(way, s))
-            def _():
-                for group in small:
-                    received(*group, way, s).wait_recv()
-                if s < steps:
-                    @pl.when(sends_on(way, s + 1))
-                    def _():
-                        for group in small:
-                            hand_on(*group, way, s + 1).start()
-
     def unpack(buf, block):
         scale = 1.0 / mass[block]
 
@@ -287,22 +226,20 @@
 
     for s in range(1, max(steps, 2)):
         forward(s)
-        if s > 1:
-            forward_small(s - 1)
-    forward_small(max(steps - 1, 1))
     for j, target in enumerate(across):
         x_copy(1 + j, lax.rem(r + n_row - 2 * (j + 1), n_row), target).wait_recv()
         x_copy(pairs + j, lax.rem(r + n_row - 2 * (j + 1), n_row), sibling).start()
     x_copy(0, sibling, sibling).wait_recv()
     for j in range(len(across)):
         x_copy(pairs + j, lax.rem(sibling + n_row - 2 * (j + 1), n_row), sibling).wait_recv()
+    for copy in (*rank_copies, *ms_copies):
+        copy.wait_recv()
     unpack(pack, c)
     for s in range(1, steps - 1):
         foreign(s)
     products(0, max(steps - 1, 1))
     if steps >= 2:
         forward(steps)
-        forward_small(steps)
     for s in range(max(steps - 1, 1), steps + 1):
         foreign(s)
     products(max(steps - 1, 1), n_col)
@@ -327,10 +264,8 @@
         for way in (0, 1):
             @pl.when(sends_on(way, s))
             def _():
-                for ch in range(CHUNKS - 1 if s == 1 else 0, CHUNKS):
+                for ch in range(CHUNKS):
                     z_copy(way, s, ch).wait_send()
-                for group in small:
-                    hand_on(*group, way, s).wait_send()
 
             @pl.when(here(way, s))
             def _():
@@ -378,12 +313,12 @@
             dma((2, steps, CHUNKS, n_layer - 1)),
             dma((n_row,)),
             dma((n_row,)),
-            dma((2, steps)),
-            dma((2, steps)),
+            dma((steps,)),
+            dma((steps,)),
             dma((n_row - 1,)),
             dma((n_row - 1,)),
-            dma((2, steps)),
-            dma((2, steps)),
+            dma((steps,)),
+            dma((steps,)),
             dma((n_row - 1,)),
             dma((n_row - 1,)),
         ],

time: 28.4 us -> 29.1 us (1.025)
  Pallas kernels: 28.2 us -> 28.9 us
    pallas_call x1, Pallas kernels: 27.3 us -> 28.1 us  [shards(): pl.pallas_call(functools.partial(kernel, dims), out_shape=(pltpu.VMEM((he...]
where the time goes in v6:
time: 29.1 us; the launch traced here: 28.9 us
  Pallas kernels  28.9 us (99%)
    pallas_call x1, Pallas kernels, shards(): pl.pallas_call(functools.partial(kernel, dims), out_shape=(pltpu.VMEM((he...  28.1 us
    pallas_call x1, Pallas kernels, shards(): pl.pallas_call(scaled, out_shape=jax.ShapeDtypeStruct((height, half), jnp...  0.83 us

profile of v6, /device:TPU:0, one launch (start us, length us, event | category | flops | bytes accessed | tf_op | source)
XLA Modules:
  0.0 28.9 jit_solution(17813229568924794528)
XLA Ops:
  0.0 28.1 %markov_step.1 = (f32[512,256]{1,0:T(8,128)S(1)}, f32[1,256]{1,0:T(1,128)S(1)}) custom-call(bf16[512,512]{1,0:T(8,128)(2,1)} %v_ref.1, s32[4,4]{1,0:T(4,128)} %m_ref.1), custom_call_target="tpu_custom_call" | custom-call | tf_op jit(solution)/shard_map/markov_step/pallas_call | solution.py:290
  28.1 0.8 %scaled.1 = f32[512,256]{1,0:T(8,128)} custom-call(f32[512,256]{1,0:T(8,128)S(1)} %get-tuple-element.7.inflated_ref, f32[1,256]{1,0:T(1,128)S(1)} %get-tuple-element.8.scale_ref), custom_call_target="tpu_custom_call" | custom-call | tf_op jit(solution)/shard_map/scaled/pallas_call | solution.py:330

commit v7 on v4

--- a/solution.py
+++ b/solution.py
@@ -48,6 +48,11 @@
     def _():
         pl.semaphore_signal(barrier, inc=1, device_id={"col": c + 1}, device_id_type=MESH)
 
+    if steps >= 2:
+        @pl.when(c == 0)
+        def _():
+            pl.semaphore_signal(barrier, inc=1, device_id={"col": steps}, device_id_type=MESH)
+
     mask_in = pltpu.make_async_copy(m_ref, mask, in_sem.at[0])
     mask_in.start()
     for t in range(tiles):
@@ -86,18 +91,9 @@
     for t in range(tiles):
         ranks[c, t // tiles_c, t % tiles_c] = own_ranks[t]
 
-    for tc in range(tiles_c):
-        total = jnp.zeros((EDGE, EDGE), jnp.float32)
-        for tr in range(tiles_r):
-            total = total + pack[own_ranks[tr * tiles_c + tc]].astype(jnp.float32)
-        mpart[r, :, tc * EDGE : (tc + 1) * EDGE] = jnp.sum(total, axis=0, keepdims=True)
-
-    for tr in range(tiles_r):
-        for j in range(half_tiles):
-            rank = ranks[c, tr, l * half_tiles + j]
-            rbuf[r, tr * EDGE : (tr + 1) * EDGE, j * EDGE : (j + 1) * EDGE] = pack[rank]
-
     neighbours = lax.select(c > 0, 1, 0) + lax.select(c + 1 < n_col, 1, 0)
+    if steps >= 2:
+        neighbours = neighbours + lax.select(c == steps, 1, 0)
     pl.semaphore_wait(barrier, n_row - 1 + n_layer - 1 + neighbours)
 
     sends = []
@@ -105,14 +101,18 @@
     def slots(layer, ch):
         return pl.ds(layer * part + ch * chunk, chunk)
 
+    def direct(way, s):
+        return way == 1 and s == steps and steps >= 2
+
     def z_copy(way, s, ch):
         bufs = from_left if way == 0 else from_right
-        src = pack if s == 1 else bufs[s - 2]
+        src = pack if s == 1 or direct(way, s) else bufs[s - 2]
+        hops = s if direct(way, s) else 1
         where = slots(l, ch)
         return pltpu.make_async_remote_copy(
             src_ref=src.at[where], dst_ref=bufs[s - 1].at[where],
             send_sem=z_send.at[way, s - 1, ch], recv_sem=z_recv.at[way, s - 1, ch],
-            device_id={"col": c + 1 if way == 0 else c - 1}, device_id_type=MESH,
+            device_id={"col": c + hops if way == 0 else c - hops}, device_id_type=MESH,
         )
 
     def y_copy(way, s, ch, j, layer):
@@ -127,11 +127,14 @@
     def here(way, s):
         return c >= s if way == 0 else c + s < n_col
 
-    def sends_on(way, s):
+    def passes_on(way, s):
         if way == 0:
             return (c + 1 < n_col) & (c >= s - 1)
         return (c >= 1) & (c + s - 1 < n_col)
 
+    def sends_on(way, s):
+        return c == steps if direct(way, s) else passes_on(way, s)
+
     def z_start(s, ch):
         for way in (0, 1):
             @pl.when(sends_on(way, s))
@@ -139,6 +142,10 @@
                 z_copy(way, s, ch).start()
 
     for ch in range(CHUNKS):
+        if steps >= 2:
+            @pl.when(sends_on(1, steps))
+            def _():
+                z_copy(1, steps, ch).start()
         z_start(1, ch)
 
     def to_peers(axis, me, size, ref, send, recv):
@@ -172,11 +179,22 @@
 
     small = ((ranks, rank_send, rank_recv), (mass, ms_send, ms_recv))
 
+    for tc in range(tiles_c):
+        total = jnp.zeros((EDGE, EDGE), jnp.float32)
+        for tr in range(tiles_r):
+            total = total + pack[own_ranks[tr * tiles_c + tc]].astype(jnp.float32)
+        mpart[r, :, tc * EDGE : (tc + 1) * EDGE] = jnp.sum(total, axis=0, keepdims=True)
+
     mp_copies = to_peers("row", r, n_row, mpart, mp_send, mp_recv)
     for way in (0, 1):
         @pl.when(sends_on(way, 1))
         def _():
             hand_on(*small[0], way, 1).start()
+
+    for tr in range(tiles_r):
+        for j in range(half_tiles):
+            rank = ranks[c, tr, l * half_tiles + j]
+            rbuf[r, tr * EDGE : (tr + 1) * EDGE, j * EDGE : (j + 1) * EDGE] = pack[rank]
 
     sibling = r + 1 - 2 * lax.rem(r, 2)
     pairs = n_row // 2
@@ -210,7 +228,7 @@
                 @pl.when(here(way, s))
                 def _():
                     z_copy(way, s, ch).wait_recv()
-                    if s < steps:
+                    if s < steps and not direct(way, s + 1):
                         @pl.when(sends_on(way, s + 1))
                         def _():
                             z_copy(way, s + 1, ch).start()
@@ -222,7 +240,7 @@
                 for group in small:
                     received(*group, way, s).wait_recv()
                 if s < steps:
-                    @pl.when(sends_on(way, s + 1))
+                    @pl.when(passes_on(way, s + 1))
                     def _():
                         for group in small:
                             hand_on(*group, way, s + 1).start()
@@ -316,6 +334,9 @@
             def _():
                 for ch in range(CHUNKS):
                     z_copy(way, s, ch).wait_send()
+
+            @pl.when(passes_on(way, s))
+            def _():
                 for group in small:
                     hand_on(*group, way, s).wait_send()
 

time: 25.8 us -> 27.3 us (1.058)
  Pallas kernels: 25.6 us -> 27.1 us
    pallas_call x1, Pallas kernels: 24.8 us -> 26.3 us  [shards(): pl.pallas_call(functools.partial(kernel, dims), out_shape=(pltpu.VMEM((he...]
where the time goes in v7:
time: 27.3 us; the launch traced here: 27.1 us
  Pallas kernels  27.1 us (99%)
    pallas_call x1, Pallas kernels, shards(): pl.pallas_call(functools.partial(kernel, dims), out_shape=(pltpu.VMEM((he...  26.3 us
    pallas_call x1, Pallas kernels, shards(): pl.pallas_call(scaled, out_shape=jax.ShapeDtypeStruct((height, half), jnp...  0.83 us

profile of v7, /device:TPU:0, one launch (start us, length us, event | category | flops | bytes accessed | tf_op | source)
XLA Modules:
  0.0 27.1 jit_solution(13091997842743462174)
XLA Ops:
  0.0 26.3 %markov_step.1 = (f32[512,256]{1,0:T(8,128)S(1)}, f32[1,256]{1,0:T(1,128)S(1)}) custom-call(bf16[512,512]{1,0:T(8,128)(2,1)} %v_ref.1, s32[4,4]{1,0:T(4,128)} %m_ref.1), custom_call_target="tpu_custom_call" | custom-call | tf_op jit(solution)/shard_map/markov_step/pallas_call | solution.py:363
  26.3 0.8 %scaled.1 = f32[512,256]{1,0:T(8,128)} custom-call(f32[512,256]{1,0:T(8,128)S(1)} %get-tuple-element.7.inflated_ref, f32[1,256]{1,0:T(1,128)S(1)} %get-tuple-element.8.scale_ref), custom_call_target="tpu_custom_call" | custom-call | tf_op jit(solution)/shard_map/scaled/pallas_call | solution.py:403

commit v8 on v4

--- a/solution.py
+++ b/solution.py
@@ -9,12 +9,12 @@
 
 MESH = pl.DeviceIdType.MESH
 EDGE = 128
-CHUNKS = 2
+CHUNKS = 1
 
 
 def kernel(
     dims, v_ref, m_ref, acc, scale_ref,
-    by_tile, pack, rbuf, left, mask, ranks, mpart, mass, wpart, *rest,
+    own, by_tile, pack, rbuf, left, mask, ranks, mpart, mass, wpart, *rest,
 ):
     n_row, n_col, n_layer, tiles_r, tiles_c, live = dims
     steps = n_col - 1
@@ -50,12 +50,8 @@
 
     mask_in = pltpu.make_async_copy(m_ref, mask, in_sem.at[0])
     mask_in.start()
-    for t in range(tiles):
-        tr, tc = t // tiles_c, t % tiles_c
-        pltpu.make_async_copy(
-            v_ref.at[tr * EDGE : (tr + 1) * EDGE, tc * EDGE : (tc + 1) * EDGE],
-            by_tile.at[t], in_sem.at[1],
-        ).start()
+    block_in = pltpu.make_async_copy(v_ref, own, in_sem.at[1])
+    block_in.start()
     zero_tile = jnp.zeros((EDGE, EDGE), jnp.bfloat16)
     for buf in (pack, *from_left):
         buf[live] = zero_tile
@@ -76,7 +72,10 @@
     for t in range(tiles):
         count = count + flags[t]
         upto.append(count)
-    pltpu.make_async_copy(by_tile, by_tile, in_sem.at[1]).wait()
+    block_in.wait()
+    for t in range(tiles):
+        tr, tc = t // tiles_c, t % tiles_c
+        by_tile[t] = own[tr * EDGE : (tr + 1) * EDGE, tc * EDGE : (tc + 1) * EDGE]
     for s in range(live):
         index = jnp.int32(0)
         for t in range(tiles - 1):
@@ -100,6 +99,19 @@
     neighbours = lax.select(c > 0, 1, 0) + lax.select(c + 1 < n_col, 1, 0)
     pl.semaphore_wait(barrier, n_row - 1 + n_layer - 1 + neighbours)
 
+    sibling = r + 1 - 2 * lax.rem(r, 2)
+    pairs = n_row // 2
+
+    def x_copy(k, section, target):
+        return pltpu.make_async_remote_copy(
+            src_ref=rbuf.at[section], dst_ref=rbuf.at[section],
+            send_sem=x_send.at[k], recv_sem=x_recv.at[k],
+            device_id={"row": target}, device_id_type=MESH,
+        )
+
+    across = [lax.rem(r + 2 * j, n_row) for j in range(1, pairs)]
+    for j, target in enumerate(across):
+        x_copy(1 + j, r, target).start()
     sends = []
 
     def slots(layer, ch):
@@ -178,19 +190,6 @@
         def _():
             hand_on(*small[0], way, 1).start()
 
-    sibling = r + 1 - 2 * lax.rem(r, 2)
-    pairs = n_row // 2
-
-    def x_copy(k, section, target):
-        return pltpu.make_async_remote_copy(
-            src_ref=rbuf.at[section], dst_ref=rbuf.at[section],
-            send_sem=x_send.at[k], recv_sem=x_recv.at[k],
-            device_id={"row": target}, device_id_type=MESH,
-        )
-
-    across = [lax.rem(r + 2 * j, n_row) for j in range(1, pairs)]
-    for j, target in enumerate(across):
-        x_copy(1 + j, r, target).start()
     x_copy(0, r, sibling).start()
 
     for copy in mp_copies:
@@ -281,28 +280,23 @@
     for j, target in enumerate(across):
         x_copy(1 + j, lax.rem(r + n_row - 2 * (j + 1), n_row), target).wait_recv()
         x_copy(pairs + j, lax.rem(r + n_row - 2 * (j + 1), n_row), sibling).start()
+    if steps >= 2:
+        forward(steps)
     x_copy(0, sibling, sibling).wait_recv()
     for j in range(len(across)):
         x_copy(pairs + j, lax.rem(sibling + n_row - 2 * (j + 1), n_row), sibling).wait_recv()
+
     unpack(pack, c)
-    for s in range(1, steps - 1):
+    for s in range(1, steps):
         foreign(s)
-    products(0, max(steps - 1, 1))
-    if steps >= 2:
-        forward(steps)
-    for s in range(max(steps - 1, 1), steps + 1):
-        foreign(s)
-    products(max(steps - 1, 1), n_col)
+    products(0, steps)
+    foreign(steps)
+    products(steps, n_col)
 
     inflated = acc[...] * acc[...]
     acc[...] = inflated
     wpart[r] = jnp.sum(inflated, axis=0, keepdims=True)
-    for copy in to_peers("row", r, n_row, wpart, w_send, w_recv):
-        copy.wait_recv()
-    total = wpart[0]
-    for j in range(1, n_row):
-        total = total + wpart[j]
-    scale_ref[...] = (height * n_row * 1.0) / total
+    w_copies = to_peers("row", r, n_row, wpart, w_send, w_recv)
 
     for copy in sends:
         copy.wait_send()
@@ -324,6 +318,13 @@
                 for ch in range(CHUNKS):
                     for j in range(1, n_layer):
                         y_copy(way, s, ch, j, l).wait_send()
+
+    for copy in w_copies:
+        copy.wait_recv()
+    total = wpart[0]
+    for j in range(1, n_row):
+        total = total + wpart[j]
+    scale_ref[...] = (height * n_row * 1.0) / total
 
 
 def scaled(inflated_ref, scale_ref, out_ref):
@@ -348,6 +349,7 @@
         in_specs=[pl.BlockSpec(memory_space=pl.ANY)] * 2,
         out_specs=(pl.BlockSpec(memory_space=pltpu.VMEM),) * 2,
         scratch_shapes=[
+            pltpu.VMEM((height, width), jnp.bfloat16),
             pltpu.VMEM((tiles_r * tiles_c, EDGE, EDGE), jnp.bfloat16),
             pltpu.VMEM((live + 1, EDGE, EDGE), jnp.bfloat16),
             pltpu.VMEM((n_row, height, half), jnp.bfloat16),

time: 25.8 us -> 30.1 us (1.17)
  Pallas kernels: 25.6 us -> 30 us
    pallas_call x1, Pallas kernels: 24.8 us -> 29.1 us  [shards(): pl.pallas_call(functools.partial(kernel, dims), out_shape=(pltpu.VMEM((he...]
where the time goes in v8:
time: 30.1 us; the launch traced here: 30 us
  Pallas kernels  30 us (100%)
    pallas_call x1, Pallas kernels, shards(): pl.pallas_call(functools.partial(kernel, dims), out_shape=(pltpu.VMEM((he...  29.1 us
    pallas_call x1, Pallas kernels, shards(): pl.pallas_call(scaled, out_shape=jax.ShapeDtypeStruct((height, half), jnp...  0.83 us

profile of v8, /device:TPU:0, one launch (start us, length us, event | category | flops | bytes accessed | tf_op | source)
XLA Modules:
  0.0 30.0 jit_solution(351812831002329268)
XLA Ops:
  0.0 29.1 %markov_step.1 = (f32[512,256]{1,0:T(8,128)S(1)}, f32[1,256]{1,0:T(1,128)S(1)}) custom-call(bf16[512,512]{1,0:T(8,128)(2,1)} %v_ref.1, s32[4,4]{1,0:T(4,128)} %m_ref.1), custom_call_target="tpu_custom_call" | custom-call | tf_op jit(solution)/shard_map/markov_step/pallas_call | solution.py:343
  29.2 0.8 %scaled.1 = f32[512,256]{1,0:T(8,128)} custom-call(f32[512,256]{1,0:T(8,128)S(1)} %get-tuple-element.7.inflated_ref, f32[1,256]{1,0:T(1,128)S(1)} %get-tuple-element.8.scale_ref), custom_call_target="tpu_custom_call" | custom-call | tf_op jit(solution)/shard_map/scaled/pallas_call | solution.py:384

commit v9 on v8

--- a/solution.py
+++ b/solution.py
@@ -9,12 +9,13 @@
 
 MESH = pl.DeviceIdType.MESH
 EDGE = 128
-CHUNKS = 1
+CHUNKS = 2
+X_CHUNKS = 4
 
 
 def kernel(
     dims, v_ref, m_ref, acc, scale_ref,
-    own, by_tile, pack, rbuf, left, mask, ranks, mpart, mass, wpart, *rest,
+    by_tile, pack, rbuf, left, mask, ranks, mpart, mass, wpart, *rest,
 ):
     n_row, n_col, n_layer, tiles_r, tiles_c, live = dims
     steps = n_col - 1
@@ -50,8 +51,12 @@
 
     mask_in = pltpu.make_async_copy(m_ref, mask, in_sem.at[0])
     mask_in.start()
-    block_in = pltpu.make_async_copy(v_ref, own, in_sem.at[1])
-    block_in.start()
+    for t in range(tiles):
+        tr, tc = t // tiles_c, t % tiles_c
+        pltpu.make_async_copy(
+            v_ref.at[tr * EDGE : (tr + 1) * EDGE, tc * EDGE : (tc + 1) * EDGE],
+            by_tile.at[t], in_sem.at[1],
+        ).start()
     zero_tile = jnp.zeros((EDGE, EDGE), jnp.bfloat16)
     for buf in (pack, *from_left):
         buf[live] = zero_tile
@@ -72,10 +77,7 @@
     for t in range(tiles):
         count = count + flags[t]
         upto.append(count)
-    block_in.wait()
-    for t in range(tiles):
-        tr, tc = t // tiles_c, t % tiles_c
-        by_tile[t] = own[tr * EDGE : (tr + 1) * EDGE, tc * EDGE : (tc + 1) * EDGE]
+    pltpu.make_async_copy(by_tile, by_tile, in_sem.at[1]).wait()
     for s in range(live):
         index = jnp.int32(0)
         for t in range(tiles - 1):
@@ -102,16 +104,24 @@
     sibling = r + 1 - 2 * lax.rem(r, 2)
     pairs = n_row // 2
 
-    def x_copy(k, section, target):
-        return pltpu.make_async_remote_copy(
-            src_ref=rbuf.at[section], dst_ref=rbuf.at[section],
-            send_sem=x_send.at[k], recv_sem=x_recv.at[k],
-            device_id={"row": target}, device_id_type=MESH,
-        )
+    x_rows = height // X_CHUNKS
+
+    def x_copies(k, section, target):
+        span = [pl.ds(q * x_rows, x_rows) for q in range(X_CHUNKS)]
+        return [
+            pltpu.make_async_remote_copy(
+                src_ref=rbuf.at[section, span[q]], dst_ref=rbuf.at[section, span[q]],
+                send_sem=x_send.at[k, q], recv_sem=x_recv.at[k, q],
+                device_id={"row": target}, device_id_type=MESH,
+            )
+            for q in range(X_CHUNKS)
+        ]
 
     across = [lax.rem(r + 2 * j, n_row) for j in range(1, pairs)]
     for j, target in enumerate(across):
-        x_copy(1 + j, r, target).start()
+        for copy in x_copies(1 + j, r, target):
+            copy.start()
+
     sends = []
 
     def slots(layer, ch):
@@ -190,7 +200,8 @@
         def _():
             hand_on(*small[0], way, 1).start()
 
-    x_copy(0, r, sibling).start()
+    for copy in x_copies(0, r, sibling):
+        copy.start()
 
     for copy in mp_copies:
         copy.wait_recv()
@@ -278,13 +289,19 @@
     for s in range(1, max(steps, 2)):
         forward(s)
     for j, target in enumerate(across):
-        x_copy(1 + j, lax.rem(r + n_row - 2 * (j + 1), n_row), target).wait_recv()
-        x_copy(pairs + j, lax.rem(r + n_row - 2 * (j + 1), n_row), sibling).start()
+        section = lax.rem(r + n_row - 2 * (j + 1), n_row)
+        for here_copy, on_copy in zip(
+            x_copies(1 + j, section, target), x_copies(pairs + j, section, sibling)
+        ):
+            here_copy.wait_recv()
+            on_copy.start()
     if steps >= 2:
         forward(steps)
-    x_copy(0, sibling, sibling).wait_recv()
+    for copy in x_copies(0, sibling, sibling):
+        copy.wait_recv()
     for j in range(len(across)):
-        x_copy(pairs + j, lax.rem(sibling + n_row - 2 * (j + 1), n_row), sibling).wait_recv()
+        for copy in x_copies(pairs + j, lax.rem(sibling + n_row - 2 * (j + 1), n_row), sibling):
+            copy.wait_recv()
 
     unpack(pack, c)
     for s in range(1, steps):
@@ -301,9 +318,10 @@
     for copy in sends:
         copy.wait_send()
     for j, target in enumerate(across):
-        x_copy(1 + j, r, target).wait_send()
-        x_copy(pairs + j, r, sibling).wait_send()
-    x_copy(0, r, sibling).wait_send()
+        for copy in (*x_copies(1 + j, r, target), *x_copies(pairs + j, r, sibling)):
+            copy.wait_send()
+    for copy in x_copies(0, r, sibling):
+        copy.wait_send()
     for s in range(1, steps + 1):
         for way in (0, 1):
             @pl.when(sends_on(way, s))
@@ -349,7 +367,6 @@
         in_specs=[pl.BlockSpec(memory_space=pl.ANY)] * 2,
         out_specs=(pl.BlockSpec(memory_space=pltpu.VMEM),) * 2,
         scratch_shapes=[
-            pltpu.VMEM((height, width), jnp.bfloat16),
             pltpu.VMEM((tiles_r * tiles_c, EDGE, EDGE), jnp.bfloat16),
             pltpu.VMEM((live + 1, EDGE, EDGE), jnp.bfloat16),
             pltpu.VMEM((n_row, height, half), jnp.bfloat16),
@@ -365,8 +382,8 @@
             dma((2, steps, CHUNKS)),
             dma((2, steps, CHUNKS, n_layer - 1)),
             dma((2, steps, CHUNKS, n_layer - 1)),
-            dma((n_row,)),
-            dma((n_row,)),
+            dma((n_row, X_CHUNKS)),
+            dma((n_row, X_CHUNKS)),
             dma((2, steps)),
             dma((2, steps)),
             dma((n_row - 1,)),

time: 30.1 us -> 29.2 us (0.970)
  Pallas kernels: 30 us -> 29 us
    pallas_call x1, Pallas kernels: 29.1 us -> 28.2 us  [shards(): pl.pallas_call(functools.partial(kernel, dims), out_shape=(pltpu.VMEM((he...]
where the time goes in v9:
time: 29.2 us; the launch traced here: 29 us
  Pallas kernels  29 us (99%)
    pallas_call x1, Pallas kernels, shards(): pl.pallas_call(functools.partial(kernel, dims), out_shape=(pltpu.VMEM((he...  28.2 us
    pallas_call x1, Pallas kernels, shards(): pl.pallas_call(scaled, out_shape=jax.ShapeDtypeStruct((height, half), jnp...  0.83 us

profile of v9, /device:TPU:0, one launch (start us, length us, event | category | flops | bytes accessed | tf_op | source)
XLA Modules:
  0.0 29.0 jit_solution(7140886787189647769)
XLA Ops:
  0.0 28.2 %markov_step.1 = (f32[512,256]{1,0:T(8,128)S(1)}, f32[1,256]{1,0:T(1,128)S(1)}) custom-call(bf16[512,512]{1,0:T(8,128)(2,1)} %v_ref.1, s32[4,4]{1,0:T(4,128)} %m_ref.1), custom_call_target="tpu_custom_call" | custom-call | tf_op jit(solution)/shard_map/markov_step/pallas_call | solution.py:361
  28.2 0.8 %scaled.1 = f32[512,256]{1,0:T(8,128)} custom-call(f32[512,256]{1,0:T(8,128)S(1)} %get-tuple-element.7.inflated_ref, f32[1,256]{1,0:T(1,128)S(1)} %get-tuple-element.8.scale_ref), custom_call_target="tpu_custom_call" | custom-call | tf_op jit(solution)/shard_map/scaled/pallas_call | solution.py:401

commit v10 on v4

--- a/solution.py
+++ b/solution.py
@@ -92,54 +92,10 @@
             total = total + pack[own_ranks[tr * tiles_c + tc]].astype(jnp.float32)
         mpart[r, :, tc * EDGE : (tc + 1) * EDGE] = jnp.sum(total, axis=0, keepdims=True)
 
-    for tr in range(tiles_r):
-        for j in range(half_tiles):
-            rank = ranks[c, tr, l * half_tiles + j]
-            rbuf[r, tr * EDGE : (tr + 1) * EDGE, j * EDGE : (j + 1) * EDGE] = pack[rank]
-
     neighbours = lax.select(c > 0, 1, 0) + lax.select(c + 1 < n_col, 1, 0)
     pl.semaphore_wait(barrier, n_row - 1 + n_layer - 1 + neighbours)
 
     sends = []
-
-    def slots(layer, ch):
-        return pl.ds(layer * part + ch * chunk, chunk)
-
-    def z_copy(way, s, ch):
-        bufs = from_left if way == 0 else from_right
-        src = pack if s == 1 else bufs[s - 2]
-        where = slots(l, ch)
-        return pltpu.make_async_remote_copy(
-            src_ref=src.at[where], dst_ref=bufs[s - 1].at[where],
-            send_sem=z_send.at[way, s - 1, ch], recv_sem=z_recv.at[way, s - 1, ch],
-            device_id={"col": c + 1 if way == 0 else c - 1}, device_id_type=MESH,
-        )
-
-    def y_copy(way, s, ch, j, layer):
-        buf = (from_left if way == 0 else from_right)[s - 1]
-        where = slots(layer, ch)
-        return pltpu.make_async_remote_copy(
-            src_ref=buf.at[where], dst_ref=buf.at[where],
-            send_sem=y_send.at[way, s - 1, ch, j - 1], recv_sem=y_recv.at[way, s - 1, ch, j - 1],
-            device_id={"layer": lax.rem(l + j, n_layer)}, device_id_type=MESH,
-        )
-
-    def here(way, s):
-        return c >= s if way == 0 else c + s < n_col
-
-    def sends_on(way, s):
-        if way == 0:
-            return (c + 1 < n_col) & (c >= s - 1)
-        return (c >= 1) & (c + s - 1 < n_col)
-
-    def z_start(s, ch):
-        for way in (0, 1):
-            @pl.when(sends_on(way, s))
-            def _():
-                z_copy(way, s, ch).start()
-
-    for ch in range(CHUNKS):
-        z_start(1, ch)
 
     def to_peers(axis, me, size, ref, send, recv):
         copies = []
@@ -154,6 +110,47 @@
             copies.append(copy)
         return copies
 
+    mp_copies = to_peers("row", r, n_row, mpart, mp_send, mp_recv)
+
+    def slots(layer, ch):
+        return pl.ds(layer * part + ch * chunk, chunk)
+
+    def z_copy(way, s, ch):
+        bufs = from_left if way == 0 else from_right
+        src = pack if s == 1 else bufs[s - 2]
+        where = slots(l, ch)
+        return pltpu.make_async_remote_copy(
+            src_ref=src.at[where], dst_ref=bufs[s - 1].at[where],
+            send_sem=z_send.at[way, s - 1, ch], recv_sem=z_recv.at[way, s - 1, ch],
+            device_id={"col": c + 1 if way == 0 else c - 1}, device_id_type=MESH,
+        )
+
+    def y_copy(way, s, ch, j, layer):
+        buf = (from_left if way == 0 else from_right)[s - 1]
+        where = slots(layer, ch)
+        return pltpu.make_async_remote_copy(
+            src_ref=buf.at[where], dst_ref=buf.at[where],
+            send_sem=y_send.at[way, s - 1, ch, j - 1], recv_sem=y_recv.at[way, s - 1, ch, j - 1],
+            device_id={"layer": lax.rem(l + j, n_layer)}, device_id_type=MESH,
+        )
+
+    def here(way, s):
+        return c >= s if way == 0 else c + s < n_col
+
+    def sends_on(way, s):
+        if way == 0:
+            return (c + 1 < n_col) & (c >= s - 1)
+        return (c >= 1) & (c + s - 1 < n_col)
+
+    def z_start(s, ch):
+        for way in (0, 1):
+            @pl.when(sends_on(way, s))
+            def _():
+                z_copy(way, s, ch).start()
+
+    for ch in range(CHUNKS):
+        z_start(1, ch)
+
     def hand_on(ref, send, recv, way, s):
         block = c - (s - 1) if way == 0 else c + (s - 1)
         return pltpu.make_async_remote_copy(
@@ -172,26 +169,15 @@
 
     small = ((ranks, rank_send, rank_recv), (mass, ms_send, ms_recv))
 
-    mp_copies = to_peers("row", r, n_row, mpart, mp_send, mp_recv)
     for way in (0, 1):
         @pl.when(sends_on(way, 1))
         def _():
             hand_on(*small[0], way, 1).start()
 
-    sibling = r + 1 - 2 * lax.rem(r, 2)
-    pairs = n_row // 2
-
-    def x_copy(k, section, target):
-        return pltpu.make_async_remote_copy(
-            src_ref=rbuf.at[section], dst_ref=rbuf.at[section],
-            send_sem=x_send.at[k], recv_sem=x_recv.at[k],
-            device_id={"row": target}, device_id_type=MESH,
-        )
-
-    across = [lax.rem(r + 2 * j, n_row) for j in range(1, pairs)]
-    for j, target in enumerate(across):
-        x_copy(1 + j, r, target).start()
-    x_copy(0, r, sibling).start()
+    for tr in range(tiles_r):
+        for j in range(half_tiles):
+            rank = ranks[c, tr, l * half_tiles + j]
+            rbuf[r, tr * EDGE : (tr + 1) * EDGE, j * EDGE : (j + 1) * EDGE] = pack[rank]
 
     for copy in mp_copies:
         copy.wait_recv()
@@ -203,6 +189,21 @@
         @pl.when(sends_on(way, 1))
         def _():
             hand_on(*small[1], way, 1).start()
+
+    sibling = r + 1 - 2 * lax.rem(r, 2)
+    pairs = n_row // 2
+
+    def x_copy(k, section, target):
+        return pltpu.make_async_remote_copy(
+            src_ref=rbuf.at[section], dst_ref=rbuf.at[section],
+            send_sem=x_send.at[k], recv_sem=x_recv.at[k],
+            device_id={"row": target}, device_id_type=MESH,
+        )
+
+    across = [lax.rem(r + 2 * j, n_row) for j in range(1, pairs)]
+    for j, target in enumerate(across):
+        x_copy(1 + j, r, target).start()
+    x_copy(0, r, sibling).start()
 
     def forward(s):
         for ch in range(CHUNKS):
@@ -297,12 +298,7 @@
     inflated = acc[...] * acc[...]
     acc[...] = inflated
     wpart[r] = jnp.sum(inflated, axis=0, keepdims=True)
-    for copy in to_peers("row", r, n_row, wpart, w_send, w_recv):
-        copy.wait_recv()
-    total = wpart[0]
-    for j in range(1, n_row):
-        total = total + wpart[j]
-    scale_ref[...] = (height * n_row * 1.0) / total
+    w_copies = to_peers("row", r, n_row, wpart, w_send, w_recv)
 
     for copy in sends:
         copy.wait_send()
@@ -324,6 +320,13 @@
                 for ch in range(CHUNKS):
                     for j in range(1, n_layer):
                         y_copy(way, s, ch, j, l).wait_send()
+
+    for copy in w_copies:
+        copy.wait_recv()
+    total = wpart[0]
+    for j in range(1, n_row):
+        total = total + wpart[j]
+    scale_ref[...] = (height * n_row * 1.0) / total
 
 
 def scaled(inflated_ref, scale_ref, out_ref):

time: 25.8 us -> 26.2 us (1.016)
  Pallas kernels: 25.6 us -> 26 us
    pallas_call x1, Pallas kernels: 24.8 us -> 25.2 us  [shards(): pl.pallas_call(functools.partial(kernel, dims), out_shape=(pltpu.VMEM((he...]
where the time goes in v10:
time: 26.2 us; the launch traced here: 26 us
  Pallas kernels  26 us (99%)
    pallas_call x1, Pallas kernels, shards(): pl.pallas_call(functools.partial(kernel, dims), out_shape=(pltpu.VMEM((he...  25.2 us
    pallas_call x1, Pallas kernels, shards(): pl.pallas_call(scaled, out_shape=jax.ShapeDtypeStruct((height, half), jnp...  0.83 us

profile of v10, /device:TPU:0, one launch (start us, length us, event | category | flops | bytes accessed | tf_op | source)
XLA Modules:
  0.0 26.0 jit_solution(1110863525897113858)
XLA Ops:
  0.0 25.2 %markov_step.1 = (f32[512,256]{1,0:T(8,128)S(1)}, f32[1,256]{1,0:T(1,128)S(1)}) custom-call(bf16[512,512]{1,0:T(8,128)(2,1)} %v_ref.1, s32[4,4]{1,0:T(4,128)} %m_ref.1), custom_call_target="tpu_custom_call" | custom-call | tf_op jit(solution)/shard_map/markov_step/pallas_call | solution.py:345
  25.2 0.8 %scaled.1 = f32[512,256]{1,0:T(8,128)} custom-call(f32[512,256]{1,0:T(8,128)S(1)} %get-tuple-element.7.inflated_ref, f32[1,256]{1,0:T(1,128)S(1)} %get-tuple-element.8.scale_ref), custom_call_target="tpu_custom_call" | custom-call | tf_op jit(solution)/shard_map/scaled/pallas_call | solution.py:385

commit v11 on v10

--- a/solution.py
+++ b/solution.py
@@ -179,6 +179,28 @@
             rank = ranks[c, tr, l * half_tiles + j]
             rbuf[r, tr * EDGE : (tr + 1) * EDGE, j * EDGE : (j + 1) * EDGE] = pack[rank]
 
+    sibling = r + 1 - 2 * lax.rem(r, 2)
+    pairs = n_row // 2
+
+    def x_copy(k, section, target):
+        return pltpu.make_async_remote_copy(
+            src_ref=rbuf.at[section], dst_ref=rbuf.at[section],
+            send_sem=x_send.at[k], recv_sem=x_recv.at[k],
+            device_id={"row": target}, device_id_type=MESH,
+        )
+
+    across = [lax.rem(r + 2 * j, n_row) for j in range(1, pairs)]
+    def x_start():
+        for j, target in enumerate(across):
+            x_copy(1 + j, r, target).start()
+        x_copy(0, r, sibling).start()
+
+    at_end = (c == 0) | (c == n_col - 1)
+
+    @pl.when(at_end)
+    def _():
+        x_start()
+
     for copy in mp_copies:
         copy.wait_recv()
     total = mpart[0]
@@ -189,21 +211,6 @@
         @pl.when(sends_on(way, 1))
         def _():
             hand_on(*small[1], way, 1).start()
-
-    sibling = r + 1 - 2 * lax.rem(r, 2)
-    pairs = n_row // 2
-
-    def x_copy(k, section, target):
-        return pltpu.make_async_remote_copy(
-            src_ref=rbuf.at[section], dst_ref=rbuf.at[section],
-            send_sem=x_send.at[k], recv_sem=x_recv.at[k],
-            device_id={"row": target}, device_id_type=MESH,
-        )
-
-    across = [lax.rem(r + 2 * j, n_row) for j in range(1, pairs)]
-    for j, target in enumerate(across):
-        x_copy(1 + j, r, target).start()
-    x_copy(0, r, sibling).start()
 
     def forward(s):
         for ch in range(CHUNKS):
@@ -279,21 +286,24 @@
 
     for s in range(1, max(steps, 2)):
         forward(s)
+        if s == 1:
+            @pl.when(jnp.logical_not(at_end))
+            def _():
+                x_start()
     for j, target in enumerate(across):
         x_copy(1 + j, lax.rem(r + n_row - 2 * (j + 1), n_row), target).wait_recv()
         x_copy(pairs + j, lax.rem(r + n_row - 2 * (j + 1), n_row), sibling).start()
+    if steps >= 2:
+        forward(steps)
     x_copy(0, sibling, sibling).wait_recv()
     for j in range(len(across)):
         x_copy(pairs + j, lax.rem(sibling + n_row - 2 * (j + 1), n_row), sibling).wait_recv()
     unpack(pack, c)
-    for s in range(1, steps - 1):
+    for s in range(1, steps):
         foreign(s)
-    products(0, max(steps - 1, 1))
-    if steps >= 2:
-        forward(steps)
-    for s in range(max(steps - 1, 1), steps + 1):
-        foreign(s)
-    products(max(steps - 1, 1), n_col)
+    products(0, steps)
+    foreign(steps)
+    products(steps, n_col)
 
     inflated = acc[...] * acc[...]
     acc[...] = inflated

time: 26.2 us -> 24.7 us (0.943)
  Pallas kernels: 26 us -> 24.5 us
    pallas_call x1, Pallas kernels: 25.2 us -> 23.7 us  [shards(): pl.pallas_call(functools.partial(kernel, dims), out_shape=(pltpu.VMEM((he...]
where the time goes in v11:
time: 24.7 us; the launch traced here: 24.5 us
  Pallas kernels  24.5 us (99%)
    pallas_call x1, Pallas kernels, shards(): pl.pallas_call(functools.partial(kernel, dims), out_shape=(pltpu.VMEM((he...  23.7 us
    pallas_call x1, Pallas kernels, shards(): pl.pallas_call(scaled, out_shape=jax.ShapeDtypeStruct((height, half), jnp...  0.83 us

profile of v11, /device:TPU:0, one launch (start us, length us, event | category | flops | bytes accessed | tf_op | source)
XLA Modules:
  0.0 24.5 jit_solution(3827195379530354993)
XLA Ops:
  0.0 23.7 %markov_step.1 = (f32[512,256]{1,0:T(8,128)S(1)}, f32[1,256]{1,0:T(1,128)S(1)}) custom-call(bf16[512,512]{1,0:T(8,128)(2,1)} %v_ref.1, s32[4,4]{1,0:T(4,128)} %m_ref.1), custom_call_target="tpu_custom_call" | custom-call | tf_op jit(solution)/shard_map/markov_step/pallas_call | solution.py:355
  23.7 0.8 %scaled.1 = f32[512,256]{1,0:T(8,128)} custom-call(f32[512,256]{1,0:T(8,128)S(1)} %get-tuple-element.7.inflated_ref, f32[1,256]{1,0:T(1,128)S(1)} %get-tuple-element.8.scale_ref), custom_call_target="tpu_custom_call" | custom-call | tf_op jit(solution)/shard_map/scaled/pallas_call | solution.py:395

commit v12 on v11

--- a/solution.py
+++ b/solution.py
@@ -193,7 +193,6 @@
     def x_start():
         for j, target in enumerate(across):
             x_copy(1 + j, r, target).start()
-        x_copy(0, r, sibling).start()
 
     at_end = (c == 0) | (c == n_col - 1)
 
@@ -290,6 +289,7 @@
             @pl.when(jnp.logical_not(at_end))
             def _():
                 x_start()
+    x_copy(0, r, sibling).start()
     for j, target in enumerate(across):
         x_copy(1 + j, lax.rem(r + n_row - 2 * (j + 1), n_row), target).wait_recv()
         x_copy(pairs + j, lax.rem(r + n_row - 2 * (j + 1), n_row), sibling).start()

time: 24.7 us -> 24.7 us (level)
  no operation moved by 1% of the time
where the time goes in v12:
time: 24.7 us; the launch traced here: 24.5 us
  Pallas kernels  24.5 us (99%)
    pallas_call x1, Pallas kernels, shards(): pl.pallas_call(functools.partial(kernel, dims), out_shape=(pltpu.VMEM((he...  23.7 us
    pallas_call x1, Pallas kernels, shards(): pl.pallas_call(scaled, out_shape=jax.ShapeDtypeStruct((height, half), jnp...  0.83 us

profile of v12, /device:TPU:0, one launch (start us, length us, event | category | flops | bytes accessed | tf_op | source)
XLA Modules:
  0.0 24.5 jit_solution(15710568357043041362)
XLA Ops:
  0.0 23.7 %markov_step.1 = (f32[512,256]{1,0:T(8,128)S(1)}, f32[1,256]{1,0:T(1,128)S(1)}) custom-call(bf16[512,512]{1,0:T(8,128)(2,1)} %v_ref.1, s32[4,4]{1,0:T(4,128)} %m_ref.1), custom_call_target="tpu_custom_call" | custom-call | tf_op jit(solution)/shard_map/markov_step/pallas_call | solution.py:355
  23.7 0.8 %scaled.1 = f32[512,256]{1,0:T(8,128)} custom-call(f32[512,256]{1,0:T(8,128)S(1)} %get-tuple-element.7.inflated_ref, f32[1,256]{1,0:T(1,128)S(1)} %get-tuple-element.8.scale_ref), custom_call_target="tpu_custom_call" | custom-call | tf_op jit(solution)/shard_map/scaled/pallas_call | solution.py:395

commit v13 on v12

--- a/solution.py
+++ b/solution.py
@@ -9,7 +9,7 @@
 
 MESH = pl.DeviceIdType.MESH
 EDGE = 128
-CHUNKS = 2
+CHUNKS = 4
 
 
 def kernel(

time: 24.7 us -> 24.1 us (0.976)
  Pallas kernels: 24.5 us -> 23.9 us
    pallas_call x1, Pallas kernels: 23.7 us -> 23.1 us  [shards(): pl.pallas_call(functools.partial(kernel, dims), out_shape=(pltpu.VMEM((he...]
where the time goes in v13:
time: 24.1 us; the launch traced here: 23.9 us
  Pallas kernels  23.9 us (99%)
    pallas_call x1, Pallas kernels, shards(): pl.pallas_call(functools.partial(kernel, dims), out_shape=(pltpu.VMEM((he...  23.1 us
    pallas_call x1, Pallas kernels, shards(): pl.pallas_call(scaled, out_shape=jax.ShapeDtypeStruct((height, half), jnp...  0.83 us

profile of v13, /device:TPU:0, one launch (start us, length us, event | category | flops | bytes accessed | tf_op | source)
XLA Modules:
  0.0 23.9 jit_solution(13223463126580403795)
XLA Ops:
  0.0 23.1 %markov_step.1 = (f32[512,256]{1,0:T(8,128)S(1)}, f32[1,256]{1,0:T(1,128)S(1)}) custom-call(bf16[512,512]{1,0:T(8,128)(2,1)} %v_ref.1, s32[4,4]{1,0:T(4,128)} %m_ref.1), custom_call_target="tpu_custom_call" | custom-call | tf_op jit(solution)/shard_map/markov_step/pallas_call | solution.py:355
  23.1 0.8 %scaled.1 = f32[512,256]{1,0:T(8,128)} custom-call(f32[512,256]{1,0:T(8,128)S(1)} %get-tuple-element.7.inflated_ref, f32[1,256]{1,0:T(1,128)S(1)} %get-tuple-element.8.scale_ref), custom_call_target="tpu_custom_call" | custom-call | tf_op jit(solution)/shard_map/scaled/pallas_call | solution.py:395

commit v14 on v13

--- a/solution.py
+++ b/solution.py
@@ -223,6 +223,10 @@
                             z_copy(way, s + 1, ch).start()
                     for j in range(1, n_layer):
                         y_copy(way, s, ch, j, l).start()
+        if s == 1:
+            @pl.when(jnp.logical_not(at_end))
+            def _():
+                x_start()
         for way in (0, 1):
             @pl.when(here(way, s))
             def _():
@@ -285,10 +289,6 @@
 
     for s in range(1, max(steps, 2)):
         forward(s)
-        if s == 1:
-            @pl.when(jnp.logical_not(at_end))
-            def _():
-                x_start()
     x_copy(0, r, sibling).start()
     for j, target in enumerate(across):
         x_copy(1 + j, lax.rem(r + n_row - 2 * (j + 1), n_row), target).wait_recv()

time: 24.1 us -> 24.1 us (level)
  no operation moved by 1% of the time
where the time goes in v14:
time: 24.1 us; the launch traced here: 23.9 us
  Pallas kernels  23.9 us (99%)
    pallas_call x1, Pallas kernels, shards(): pl.pallas_call(functools.partial(kernel, dims), out_shape=(pltpu.VMEM((he...  23.1 us
    pallas_call x1, Pallas kernels, shards(): pl.pallas_call(scaled, out_shape=jax.ShapeDtypeStruct((height, half), jnp...  0.83 us

profile of v14, /device:TPU:0, one launch (start us, length us, event | category | flops | bytes accessed | tf_op | source)
XLA Modules:
  0.0 23.9 jit_solution(15575746424897648695)
XLA Ops:
  0.0 23.1 %markov_step.1 = (f32[512,256]{1,0:T(8,128)S(1)}, f32[1,256]{1,0:T(1,128)S(1)}) custom-call(bf16[512,512]{1,0:T(8,128)(2,1)} %v_ref.1, s32[4,4]{1,0:T(4,128)} %m_ref.1), custom_call_target="tpu_custom_call" | custom-call | tf_op jit(solution)/shard_map/markov_step/pallas_call | solution.py:355
  23.1 0.8 %scaled.1 = f32[512,256]{1,0:T(8,128)} custom-call(f32[512,256]{1,0:T(8,128)S(1)} %get-tuple-element.7.inflated_ref, f32[1,256]{1,0:T(1,128)S(1)} %get-tuple-element.8.scale_ref), custom_call_target="tpu_custom_call" | custom-call | tf_op jit(solution)/shard_map/scaled/pallas_call | solution.py:395

commit v15 on v14

--- a/solution.py
+++ b/solution.py
@@ -10,6 +10,7 @@
 MESH = pl.DeviceIdType.MESH
 EDGE = 128
 CHUNKS = 4
+X_CHUNKS = 2
 
 
 def kernel(
@@ -182,23 +183,27 @@
     sibling = r + 1 - 2 * lax.rem(r, 2)
     pairs = n_row // 2
 
-    def x_copy(k, section, target):
+    x_rows = height // X_CHUNKS
+
+    def x_copy(k, section, target, q):
+        rows = pl.ds(q * x_rows, x_rows)
         return pltpu.make_async_remote_copy(
-            src_ref=rbuf.at[section], dst_ref=rbuf.at[section],
-            send_sem=x_send.at[k], recv_sem=x_recv.at[k],
+            src_ref=rbuf.at[section, rows], dst_ref=rbuf.at[section, rows],
+            send_sem=x_send.at[k, q], recv_sem=x_recv.at[k, q],
             device_id={"row": target}, device_id_type=MESH,
         )
 
     across = [lax.rem(r + 2 * j, n_row) for j in range(1, pairs)]
-    def x_start():
+    def x_start(q):
         for j, target in enumerate(across):
-            x_copy(1 + j, r, target).start()
+            x_copy(1 + j, r, target, q).start()
 
     at_end = (c == 0) | (c == n_col - 1)
 
     @pl.when(at_end)
     def _():
-        x_start()
+        for q in range(X_CHUNKS):
+            x_start(q)
 
     for copy in mp_copies:
         copy.wait_recv()
@@ -223,10 +228,11 @@
                             z_copy(way, s + 1, ch).start()
                     for j in range(1, n_layer):
                         y_copy(way, s, ch, j, l).start()
-        if s == 1:
+        if s <= X_CHUNKS and s < steps:
             @pl.when(jnp.logical_not(at_end))
             def _():
-                x_start()
+                for q in range(s - 1, X_CHUNKS if s == min(X_CHUNKS, steps - 1) else s):
+                    x_start(q)
         for way in (0, 1):
             @pl.when(here(way, s))
             def _():
@@ -289,15 +295,20 @@
 
     for s in range(1, max(steps, 2)):
         forward(s)
-    x_copy(0, r, sibling).start()
-    for j, target in enumerate(across):
-        x_copy(1 + j, lax.rem(r + n_row - 2 * (j + 1), n_row), target).wait_recv()
-        x_copy(pairs + j, lax.rem(r + n_row - 2 * (j + 1), n_row), sibling).start()
+    for q in range(X_CHUNKS):
+        x_copy(0, r, sibling, q).start()
+    for q in range(X_CHUNKS):
+        for j, target in enumerate(across):
+            section = lax.rem(r + n_row - 2 * (j + 1), n_row)
+            x_copy(1 + j, section, target, q).wait_recv()
+            x_copy(pairs + j, section, sibling, q).start()
     if steps >= 2:
         forward(steps)
-    x_copy(0, sibling, sibling).wait_recv()
-    for j in range(len(across)):
-        x_copy(pairs + j, lax.rem(sibling + n_row - 2 * (j + 1), n_row), sibling).wait_recv()
+    for q in range(X_CHUNKS):
+        x_copy(0, sibling, sibling, q).wait_recv()
+        for j in range(len(across)):
+            section = lax.rem(sibling + n_row - 2 * (j + 1), n_row)
+            x_copy(pairs + j, section, sibling, q).wait_recv()
     unpack(pack, c)
     for s in range(1, steps):
         foreign(s)
@@ -312,10 +323,11 @@
 
     for copy in sends:
         copy.wait_send()
-    for j, target in enumerate(across):
-        x_copy(1 + j, r, target).wait_send()
-        x_copy(pairs + j, r, sibling).wait_send()
-    x_copy(0, r, sibling).wait_send()
+    for q in range(X_CHUNKS):
+        for j, target in enumerate(across):
+            x_copy(1 + j, r, target, q).wait_send()
+            x_copy(pairs + j, r, sibling, q).wait_send()
+        x_copy(0, r, sibling, q).wait_send()
     for s in range(1, steps + 1):
         for way in (0, 1):
             @pl.when(sends_on(way, s))
@@ -376,8 +388,8 @@
             dma((2, steps, CHUNKS)),
             dma((2, steps, CHUNKS, n_layer - 1)),
             dma((2, steps, CHUNKS, n_layer - 1)),
-            dma((n_row,)),
-            dma((n_row,)),
+            dma((n_row, X_CHUNKS)),
+            dma((n_row, X_CHUNKS)),
             dma((2, steps)),
             dma((2, steps)),
             dma((n_row - 1,)),

time: 24.1 us -> 24.2 us (level)
  no operation moved by 1% of the time
where the time goes in v15:
time: 24.2 us; the launch traced here: 24 us
  Pallas kernels  24 us (99%)
    pallas_call x1, Pallas kernels, shards(): pl.pallas_call(functools.partial(kernel, dims), out_shape=(pltpu.VMEM((he...  23.1 us
    pallas_call x1, Pallas kernels, shards(): pl.pallas_call(scaled, out_shape=jax.ShapeDtypeStruct((height, half), jnp...  0.83 us

profile of v15, /device:TPU:0, one launch (start us, length us, event | category | flops | bytes accessed | tf_op | source)
XLA Modules:
  0.0 24.0 jit_solution(11967236965638826074)
XLA Ops:
  0.0 23.1 %markov_step.1 = (f32[512,256]{1,0:T(8,128)S(1)}, f32[1,256]{1,0:T(1,128)S(1)}) custom-call(bf16[512,512]{1,0:T(8,128)(2,1)} %v_ref.1, s32[4,4]{1,0:T(4,128)} %m_ref.1), custom_call_target="tpu_custom_call" | custom-call | tf_op jit(solution)/shard_map/markov_step/pallas_call | solution.py:367
  23.2 0.8 %scaled.1 = f32[512,256]{1,0:T(8,128)} custom-call(f32[512,256]{1,0:T(8,128)S(1)} %get-tuple-element.7.inflated_ref, f32[1,256]{1,0:T(1,128)S(1)} %get-tuple-element.8.scale_ref), custom_call_target="tpu_custom_call" | custom-call | tf_op jit(solution)/shard_map/scaled/pallas_call | solution.py:407
